TPU v7x, 128 devices: a whole 4x4x4 slice. The times are simulated.
128 devices in a mesh: ctx: 32 (over x, y_lo, z), tp: 4 (over y_hi, core).
Axes of the slice: x: 4, y: 4 (y_hi: 2, y_lo: 2; y = y_hi * 2 + y_lo), z: 4, core: 2. Of those that a mesh axis runs over, the one named last changes fastest.
Arguments:
- stream_in: bfloat16 [4096, 6144], P(('ctx', 'tp')), may hold values from -3 to 3
- queries: bfloat16 [4096, 3072], P('ctx', 'tp'), may hold values from -5 to 5
- rotated_key_heads: bfloat16 [4096, 512], P('ctx', 'tp'), may hold values from -5 to 5
- values: bfloat16 [4096, 512], P('ctx', 'tp'), may hold values from -6 to 6
- doc_ids: int32 [4096], P('ctx'), may hold values from 0 to 7, never falling along the last dimension, each value on 1 to 2048 neighbouring positions
- out_proj: bfloat16 [3072, 6144], P('tp', 'ctx'), may hold values from -0.4375 to 0.4375
- norm_gain: float32 [6144], replicated, may hold values from 0.1 to 1.9
- router: float32 [6144, 8], replicated, may hold values from -0.078125 to 0.078125
- w_gate: bfloat16 [6144, 65536], P(None, ('ctx', 'tp')), may hold values from -0.078125 to 0.078125
- w_up: bfloat16 [6144, 65536], P(None, ('ctx', 'tp')), may hold values from -0.078125 to 0.078125
- w_down: bfloat16 [65536, 6144], P(('ctx', 'tp')), may hold values from -0.0625 to 0.0625
- routes: int32 [4096, 2], P(('ctx', 'tp')), may hold values from 0 to 7, all different within a row; in each aligned block of 32 rows (0 to 31, 32 to 63, ...) at most 9 rows name the same one
Outputs:
- layer_out: bfloat16 [4096, 6144], P(('ctx', 'tp'))
Inputs may be any that keep to these rules, and one draw needn't show every extreme that they name: `doc_ids`: starts at 0 and never falls; each document holds 1 to 2048 positions, and one holds exactly 2048. `routes`: each row names two different experts; in each aligned block of 32 rows (the rows of one device) no expert is named by more than 9 rows, and in every draw some block names some expert exactly 9 times.
All inputs are finite; a program needn't handle non-finite values.
Results may differ from a plain program's by a relative error of at most 0.019.
Values may be sent and summed in bfloat16 or wider, within the bound.
No kernel may reach another device: no remote copies, remote signals or barrier semaphores. Data moves between devices by JAX's collectives and lax.ppermute only.
A program may use at most 192 MiB of HBM per device.

v0:
```python
import jax
import jax.numpy as jnp
from jax import lax
from jax.sharding import PartitionSpec as P

HEAD_WIDTH = 128


def per_device(
    stream_in,
    queries,
    rotated_key_heads,
    values,
    doc_ids,
    out_proj,
    norm_gain,
    router,
    w_gate,
    w_up,
    w_down,
    routes,
):
    ctx_count = lax.axis_size("ctx")
    tp_count = lax.axis_size("tp")
    tok = queries.shape[0]
    kv_local = rotated_key_heads.shape[1] // HEAD_WIDTH
    q_local = queries.shape[1] // HEAD_WIDTH
    group_size = q_local // kv_local
    scale = HEAD_WIDTH ** (-0.5)
    query_four = queries.reshape(tok, kv_local, group_size, HEAD_WIDTH)
    query_place = lax.axis_index("ctx") * tok + jnp.arange(tok, dtype=jnp.int32)
    highest = jnp.full((kv_local, group_size, tok), -1e30, jnp.float32)
    key_piece = lax.all_gather(rotated_key_heads, "ctx", axis=0, tiled=True)
    value_piece = lax.all_gather(values, "ctx", axis=0, tiled=True)
    doc_piece = lax.all_gather(doc_ids, "ctx", axis=0, tiled=True)
    count = key_piece.shape[0]
    key_three = key_piece.reshape(count, kv_local, HEAD_WIDTH)
    value_three = value_piece.reshape(count, kv_local, HEAD_WIDTH)
    scores = (
        jnp.einsum("tkgd,pkd->kgtp", query_four, key_three, preferred_element_type=jnp.float32)
        * scale
    )
    key_place = jnp.arange(count, dtype=jnp.int32)
    allowed = (key_place[None, :] <= query_place[:, None]) & (
        doc_ids[:, None] == doc_piece[None, :]
    )
    masked = jnp.where(allowed, scores, -1e30)
    new_high = jnp.maximum(highest, jnp.max(masked, axis=-1))
    expo = jnp.where(allowed, jnp.exp(scores - new_high[..., None]), 0.0)
    total = jnp.sum(expo, axis=-1)
    accum = jnp.einsum(
        "kgtp,pkd->kgtd", expo.astype(jnp.bfloat16), value_three, preferred_element_type=jnp.float32
    )
    highest, total, accum = (new_high, total, accum)
    heads_out = (
        (accum / total[..., None])
        .transpose(2, 0, 1, 3)
        .reshape(tok, q_local * HEAD_WIDTH)
        .astype(jnp.bfloat16)
    )
    partial_value = jnp.dot(
        heads_out,
        lax.all_gather(out_proj, "ctx", axis=1, tiled=True),
        preferred_element_type=jnp.float32,
    )
    summed = lax.psum_scatter(
        partial_value.astype(jnp.bfloat16), "tp", scatter_dimension=0, tiled=True
    ).astype(jnp.float32)
    resid = stream_in.astype(jnp.float32) + summed
    width = resid.shape[1]
    normed = (
        resid * lax.rsqrt(jnp.mean(resid * resid, axis=1, keepdims=True) + 1e-05) * norm_gain
    ).astype(jnp.bfloat16)
    logits = jnp.dot(normed.astype(jnp.float32), router, precision=lax.Precision.HIGHEST)
    experts = router.shape[1]
    rows = normed.shape[0]
    slot_cap = rows * 9 // 32
    per_expert_ctx = ctx_count // experts
    hits = routes[:, :, None] == jnp.arange(experts, dtype=jnp.int32)
    flat_hits = hits.astype(jnp.int32).reshape(rows * 2, experts)
    before = jnp.cumsum(flat_hits, axis=0) - flat_hits
    slot = jnp.sum(before.reshape(rows, 2, experts) * hits.astype(jnp.int32), axis=-1)
    target = routes * slot_cap + slot
    slot_ids = jnp.arange(experts * slot_cap, dtype=jnp.int32)
    placed = target[:, :, None] == slot_ids[None, None, :]
    chooser = jnp.any(placed, axis=1).astype(jnp.bfloat16).T
    packed = jnp.dot(chooser, normed, preferred_element_type=jnp.float32).astype(jnp.bfloat16)
    pair_logits = jnp.sum(jnp.where(hits, logits[:, None, :], 0.0), axis=-1)
    first_gate = 1.0 / (1.0 + jnp.exp(pair_logits[:, 1] - pair_logits[:, 0]))
    second_gate = 1.0 / (1.0 + jnp.exp(pair_logits[:, 0] - pair_logits[:, 1]))
    gate_pair = jnp.stack([first_gate, second_gate], axis=1)
    combiner = jnp.sum(jnp.where(placed, gate_pair[:, :, None], 0.0), axis=1)
    outgoing = jnp.broadcast_to(
        packed.reshape(experts, 1, slot_cap, width),
        (experts, per_expert_ctx * tp_count, slot_cap, width),
    ).reshape(-1, slot_cap, width)
    block = lax.all_to_all(outgoing, ("ctx", "tp"), split_axis=0, concat_axis=0, tiled=True)
    flat_rows = block.reshape(-1, block.shape[-1])
    gate_val = jnp.dot(flat_rows, w_gate, preferred_element_type=jnp.float32)
    up_val = jnp.dot(flat_rows, w_up, preferred_element_type=jnp.float32)
    hidden = (jax.nn.silu(gate_val) * up_val).astype(jnp.bfloat16)
    result = jnp.dot(hidden, w_down, preferred_element_type=jnp.float32)
    worked = result.reshape(block.shape[:-1] + (w_down.shape[1],))
    worked = worked.reshape(ctx_count, tp_count, slot_cap, width)
    grouped = lax.psum_scatter(
        worked.astype(jnp.bfloat16), "tp", scatter_dimension=1, tiled=True
    ).astype(jnp.float32)
    grouped = grouped.reshape(ctx_count, slot_cap, width).astype(jnp.bfloat16)
    returned = lax.all_to_all(grouped, "ctx", split_axis=0, concat_axis=0, tiled=True)
    per_expert = jnp.sum(
        returned.reshape(experts, per_expert_ctx, slot_cap, width).astype(jnp.float32), axis=1
    )
    per_expert = per_expert.reshape(experts * slot_cap, width)
    mixture = jnp.dot(combiner, per_expert, precision=lax.Precision.HIGHEST)
    return (resid + mixture).astype(jnp.bfloat16)


def solution(mesh):
    placed = (
        P(("ctx", "tp"), None),
        P("ctx", "tp"),
        P("ctx", "tp"),
        P("ctx", "tp"),
        P("ctx"),
        P("tp", "ctx"),
        P(),
        P(),
        P(None, ("ctx", "tp")),
        P(None, ("ctx", "tp")),
        P(("ctx", "tp"), None),
        P(("ctx", "tp"), None),
    )
    return jax.shard_map(
        per_device, mesh=mesh, in_specs=placed, out_specs=P(("ctx", "tp"), None), check_vma=False
    )
```

profile of v0, /device:TPU:1, one launch (start us, length us, event | category | flops | bytes accessed | tf_op | source)
XLA Modules:
  0.0 1140.3 jit_solution(7536114861962801162)
XLA Ops:
  6.5 0.0 copy-start
  6.5 0.0 all-gather.5.cloned.1.call-start
  6.5 0.7 all-gather.5.cloned.1.call-update
  7.3 0.0 all-gather.7.cloned.1.call-start
  7.3 1.5 copy.69
  8.8 0.0 all-gather.7.cloned.1.call-update
  8.8 0.0 all-gather.9.cloned.1.call-start
  8.9 0.7 all-gather.9.cloned.1.call-update
  9.5 0.0 reduce-scatter.3.cloned.1.call-start
  9.6 1.1 copy.67
  10.7 69.6 %all-gather = s32[32,1,128]{2,1,0:T(1,128)S(1)} all-gather(s32[1,1,128]{2,1,0:T(1,128)} %bitcast.71), channel_id=1, replica_groups=mesh['ctx'=32,'tp'=4] {'ctx'}, dimensions={0}, use_global_device_ids=true | all-gather | bytes 16896 | tf_op jit(solution)/shard_map/all_gather | solution.py:35
  80.3 2.5 fusion.16
  82.8 59.0 %all-gather.5.cloned.1.call-done = bf16[4096,128]{1,0:T(8,128)(2,1)} async-done(((bf16[128,128]{1,0:T(8,128)(2,1)}), bf16[4096,128]{1,0:T(8,128)(2,1)}) %all-gather.5.cloned.1.call-update) | async-done | bytes 1048592 | tf_op jit(solution)/shard_map/all_gather | solution.py:33
  141.8 3.2 fusion
  145.0 0.0 copy-start.1
  145.0 4.5 copy-done.1
  149.6 2.6 fusion.3
  152.2 116.1 %all-gather.7.cloned.1.call-done = bf16[4096,128]{0,1:T(8,128)(2,1)} async-done(((bf16[128,128]{0,1:T(8,128)(2,1)}), bf16[4096,128]{0,1:T(8,128)(2,1)}) %all-gather.7.cloned.1.call-update) | async-done | bytes 1048592 | tf_op jit(solution)/shard_map/all_gather | solution.py:34
  268.3 7.5 fusion.26
  275.8 160.4 %all-gather.9.cloned.1.call-done = bf16[768,6144]{0,1:T(8,128)(2,1)} async-done(((bf16[768,192]{0,1:T(8,128)(2,1)}), bf16[768,6144]{0,1:T(8,128)(2,1)}) %all-gather.9.cloned.1.call-update) | async-done | bytes 9437200 | tf_op jit(solution)/shard_map/all_gather | solution.py:63
  436.2 0.0 copy-start.5
  436.2 0.0 copy-start.2
  436.2 0.0 copy-start.4
  436.2 8.1 convolution_convert_fusion.1
  444.3 0.0 reduce-scatter.3.cloned.1.call-update
  444.3 0.0 reduce-scatter.5.cloned.1.call-start
  444.4 0.0 copy-done.5
  444.4 0.1 copy.71
  444.5 0.1 eq.54
  444.6 0.1 fusion.32
  444.6 0.1 reduce_window_sum.11
  444.7 0.2 select_reduce_fusion.1
  444.9 0.1 reduce_sum.58
  445.0 0.1 copy.72
  445.1 0.1 fusion.31
  445.2 54.0 %reduce-scatter.3.cloned.1.call-done = bf16[32,6144]{1,0:T(8,128)(2,1)} async-done(((bf16[128,6144]{1,0:T(8,128)(2,1)}), bf16[32,6144]{1,0:T(8,128)(2,1)}) %reduce-scatter.3.cloned.1.call-update) | async-done | bytes 393232 | tf_op jit(solution)/shard_map/reduce_scatter | solution.py:66
  499.2 0.0 copy-done.2
  499.2 1.2 multiply_reduce_fusion
  500.4 0.0 copy-done.4
  500.4 1.4 convolution_convert_fusion.2
  501.9 0.4 broadcast_in_dim.68
  502.3 3.2 broadcast_in_dim.69
  505.5 304.6 %all_to_all.10 = bf16[128,9,6144]{2,1,0:T(8,128)(2,1)} all-to-all(bf16[128,9,6144]{2,1,0:T(8,128)(2,1)S(1)} %bitcast.66), channel_id=1, replica_groups=mesh['ctx'=32,'tp'=4] {'ctx','tp'}, dimensions={0} | all-to-all | bytes 28311552 | tf_op jit(solution)/shard_map/all_to_all | solution.py:97
  810.1 20.7 %reshape.92 = bf16[1152,6144]{1,0:T(8,128)(2,1)} reshape(bf16[128,9,6144]{2,1,0:T(8,128)(2,1)} %all_to_all.10) | data formatting | bytes 28311552 | tf_op jit(solution)/shard_map/reshape | solution.py:98
  830.8 13.5 %fusion.37 = f32[1152,512]{1,0:T(8,128)} fusion(bf16[1152,6144]{1,0:T(8,128)(2,1)} %reshape.92, bf16[6144,512]{1,0:T(8,128)(2,1)} %param.20), kind=kOutput, calls=%fused_computation.53 | convolution fusion | flops 7247757312 | bytes 22806528 | tf_op jit(solution)/shard_map/dot_general | solution.py:99
  844.3 23.9 %convolution_convert_fusion = bf16[1152,6144]{1,0:T(8,128)(2,1)} fusion(bf16[512,6144]{1,0:T(8,128)(2,1)} %param.22, bf16[1152,6144]{1,0:T(8,128)(2,1)} %reshape.92, bf16[6144,512]{1,0:T(8,128)(2,1)} %param.21, f32[1152,512]{1,0:T(8,128)} %fusion.37), kind=kOutput, calls=%fused_computation | convolution fusion | flops 14506131456 | bytes 43253760 | tf_op jit(solution)/shard_map/dot_general | solution.py:102
  868.2 19.4 %convert_element_type.75 = bf16[32,4,9,6144]{3,2,1,0:T(8,128)(2,1)} reshape(bf16[1152,6144]{1,0:T(8,128)(2,1)} %convolution_convert_fusion) | data formatting | bytes 28311552 | tf_op jit(solution)/shard_map/convert_element_type | solution.py:106
  887.6 18.9 %copy.73 = bf16[32,4,9,6144]{3,0,2,1:T(8,128)(2,1)} copy(bf16[32,4,9,6144]{3,2,1,0:T(8,128)(2,1)} %convert_element_type.75) | data formatting | bytes 28311552 | tf_op jit(solution)/shard_map/convert_element_type | solution.py:106
  906.5 0.0 reduce-scatter.5.cloned.1.call-update
  906.5 119.6 %reduce-scatter.5.cloned.1.call-done = bf16[32,1,9,6144]{3,0,2,1:T(8,128)(2,1)} async-done(((bf16[32,4,9,6144]{3,0,2,1:T(8,128)(2,1)}), bf16[32,1,9,6144]{3,0,2,1:T(8,128)(2,1)}) %reduce-scatter.5.cloned.1.call-update) | async-done | bytes 3538960 | tf_op jit(solution)/shard_map/reduce_scatter | solution.py:105
  1026.1 6.9 copy.74
  1033.0 0.0 copy-start.3
  1033.0 7.2 all-to-all-start.1
  1040.2 0.0 copy-done
  1040.2 0.0 copy-done.3
  1040.3 0.5 fusion.36
  1040.8 0.1 select_reduce_fusion
  1040.9 83.8 %all-to-all-done.1 = bf16[32,9,6144]{2,1,0:T(8,128)(2,1)} async-done(((bf16[32,9,6144]{2,1,0:T(8,128)(2,1)}), bf16[32,9,6144]{2,1,0:T(8,128)(2,1)}, u32[]{:S(2)}, u32[]{:S(2)}) %all-to-all-start.1) | async-done | bytes 3538976 | tf_op jit(solution)/shard_map/all_to_all | solution.py:109
  1124.7 4.2 convert_reduce_fusion
  1128.9 1.5 reshape.93
  1130.4 3.4 fusion.5
  (7 shorter events, 0.1 us)
Async XLA Ops:
  6.5 1033.7 %copy-start = (f32[6144,8]{0,1:T(8,128)S(1)}, f32[6144,8]{0,1:T(8,128)}, u32[]{:S(2)}) copy-start(f32[6144,8]{0,1:T(8,128)} %param.19) | copy-start | bytes 589828
  6.5 135.3 %all-gather.5.cloned.1.call-start = ((), (), s32[]{:S(2)}) async-start(), calls=%async_computation.4 | async-start | bytes 1081344 | tf_op jit(solution)/shard_map/all_gather | solution.py:33
  7.3 261.0 %all-gather.7.cloned.1.call-start = ((), (), s32[]{:S(2)}) async-start(), calls=%async_computation.5 | async-start | bytes 1081344 | tf_op jit(solution)/shard_map/all_gather | solution.py:34
  8.8 427.4 %all-gather.9.cloned.1.call-start = ((), (), s32[]{:S(2)}) async-start(), calls=%async_computation.6 | async-start | bytes 9732096 | tf_op jit(solution)/shard_map/all_gather | solution.py:63
  9.5 489.7 %reduce-scatter.3.cloned.1.call-start = ((), (), s32[]{:S(2)}) async-start(), calls=%async_computation.7 | async-start | bytes 1966080 | tf_op jit(solution)/shard_map/reduce_scatter | solution.py:66
  145.0 4.6 copy-start.1
  436.2 8.2 copy-start.5
  436.2 63.0 %copy-start.2 = (bf16[32,6144]{1,0:T(8,128)(2,1)S(1)}, bf16[32,6144]{1,0:T(8,128)(2,1)}, u32[]{:S(2)}) copy-start(bf16[32,6144]{1,0:T(8,128)(2,1)} %param.12) | copy-start | bytes 1179652
  436.2 64.2 %copy-start.4 = (f32[6144]{0:T(1024)S(1)}, f32[6144]{0:T(1024)}, u32[]{:S(2)}) copy-start(f32[6144]{0:T(1024)} %param.18) | copy-start | bytes 73732
  444.3 581.8 %reduce-scatter.5.cloned.1.call-start = ((), (), s32[]{:S(2)}) async-start(), calls=%async_computation.8 | async-start | bytes 17694720 | tf_op jit(solution)/shard_map/reduce_scatter | solution.py:105
  1033.0 7.2 copy-start.3
  1033.0 91.6 %all-to-all-start.1 = ((bf16[32,9,6144]{2,1,0:T(8,128)(2,1)}), bf16[32,9,6144]{2,1,0:T(8,128)(2,1)}, u32[]{:S(2)}, u32[]{:S(2)}) async-start(bf16[32,9,6144]{2,1,0:T(8,128)(2,1)} %copy.74), calls=%async_computation.3 | async-start | bytes 12582912 | tf_op jit(solution)/shard_map/all_to_all | solution.py:109
Sparse Core Ops, SparseCore 0:
  9.0 132.7 all-gather.4
  143.4 124.8 all-gather.6
  269.9 166.2 all-gather.8
  444.4 54.7 reduce-scatter.2
  906.6 119.4 reduce-scatter.4
where the time goes:
time: 1140 us
  waiting for transfers between devices  594 us (52%)
  blocking collectives  374 us (33%)
  local copies, waits for them, and re-layouts  78.5 us (7%)
  matrix products  61.5 us (5%)
  between operations  13.3 us (1%)
    all_to_all x1, blocking collectives, per_device(): lax.all_to_all(outgoing, ('ctx', 'tp'), split_axis=0, concat_axis=0, tile...  305 us
    all_gather x1, waiting for transfers between devices, per_device(): lax.all_gather(out_proj, 'ctx', axis=1, tiled=True)  160 us
    reduce_scatter x1, waiting for transfers between devices, per_device(): lax.psum_scatter(worked.astype(jnp.bfloat16), 'tp', scatter_dimension=1,...  120 us
    all_gather x1, waiting for transfers between devices, per_device(): value_piece = lax.all_gather(values, 'ctx', axis=0, tiled=True)  116 us
    all_to_all x1, waiting for transfers between devices, per_device(): lax.all_to_all(grouped, 'ctx', split_axis=0, concat_axis=0, tiled=True)  83.8 us
    all_gather x1, blocking collectives, per_device(): doc_piece = lax.all_gather(doc_ids, 'ctx', axis=0, tiled=True)  69.6 us
    all_gather x1, waiting for transfers between devices, per_device(): key_piece = lax.all_gather(rotated_key_heads, 'ctx', axis=0, tiled=True)  59 us
    reduce_scatter x1, waiting for transfers between devices, per_device(): lax.psum_scatter(partial_value.astype(jnp.bfloat16), 'tp', scatter_dimens...  54 us
  transfers between devices with their start and end apart: 6, of which 6 were waited for; matrix products, arithmetic and copies ran while one was open for 2% of the time, Pallas kernels for 0%

commit v1 on v0

v1 whole, which is shorter than its diff:
```python
import jax
import jax.numpy as jnp
from jax import lax
from jax.sharding import Mesh, PartitionSpec as P

HEAD_WIDTH = 128
LONGEST = 2048
GROUPS = 8
NX, NYL, NZ, NYH, NC = 4, 2, 4, 2, 2
SWAP = [(0, 1), (1, 0)]
UP = [(i, (i + 1) % NZ) for i in range(NZ)]
DOWN = [((i + 1) % NZ, i) for i in range(NZ)]


def add(*terms):
    total = terms[0].astype(jnp.float32)
    for term in terms[1:]:
        total = total + term.astype(jnp.float32)
    return total.astype(jnp.bfloat16)


def gather_keys(keys, values, doc_ids):
    tok = keys.shape[0]
    docs = jnp.pad(doc_ids.astype(jnp.bfloat16)[None, :], ((0, 15), (0, 0)))
    own = jnp.concatenate([keys, values, docs], axis=0)
    one = lax.ppermute(own, "x", [(i, i + 1) for i in range(NX - 1)])
    two = lax.ppermute(own, "x", [(i, i + 2) for i in range(NX - 2)])
    mine = jnp.concatenate([own, one, two], axis=0)
    other = lax.ppermute(mine, "yl", SWAP)
    here = jnp.concatenate([mine, other], axis=0)
    below = lax.ppermute(here, "z", UP)
    above = lax.ppermute(here, "z", DOWN)
    half = here.shape[0] // 2
    far_first = lax.ppermute(below[:half], "z", UP)
    far_second = lax.ppermute(above[half:], "z", DOWN)
    blocks = jnp.concatenate([here, below, above, far_first, far_second], axis=0)
    blocks = blocks.reshape(NZ, NYL, 3, own.shape[0], HEAD_WIDTH)
    x, yl, z = lax.axis_index("x"), lax.axis_index("yl"), lax.axis_index("z")
    at_x = x - jnp.arange(3, dtype=jnp.int32)
    at_yl = jnp.stack([yl, 1 - yl])
    at_z = (z + jnp.array([0, 3, 1, 2], jnp.int32)) % NZ
    base = (at_x[None, None, :] * NYL + at_yl[None, :, None]) * NZ + at_z[:, None, None]
    place = base[..., None] * tok + jnp.arange(tok, dtype=jnp.int32)
    place = jnp.where(at_x[None, None, :, None] >= 0, place, 1 << 30)
    key_all = blocks[..., :tok, :].reshape(-1, HEAD_WIDTH)
    value_all = blocks[..., tok : 2 * tok, :].reshape(-1, HEAD_WIDTH)
    doc_all = blocks[..., 2 * tok, :].astype(jnp.int32).reshape(-1)
    return key_all, value_all, doc_all, place.reshape(-1)


def attention(queries, keys, values, doc_ids):
    tok = queries.shape[0]
    heads = queries.shape[1] // HEAD_WIDTH
    key_all, value_all, doc_all, key_place = gather_keys(keys, values, doc_ids)
    ctx = (lax.axis_index("x") * NYL + lax.axis_index("yl")) * NZ + lax.axis_index("z")
    query_place = ctx * tok + jnp.arange(tok, dtype=jnp.int32)
    allowed = (key_place[None, :] <= query_place[:, None]) & (doc_ids[:, None] == doc_all[None, :])
    query_three = queries.reshape(tok, heads, HEAD_WIDTH)
    scores = jnp.einsum(
        "tgd,pd->gtp", query_three, key_all, preferred_element_type=jnp.float32
    ) * (HEAD_WIDTH ** (-0.5))
    masked = jnp.where(allowed, scores, -1e30)
    top = jnp.max(masked, axis=-1, keepdims=True)
    expo = jnp.where(allowed, jnp.exp(scores - top), 0.0)
    total = jnp.sum(expo, axis=-1)
    accum = jnp.einsum(
        "gtp,pd->gtd", expo.astype(jnp.bfloat16), value_all, preferred_element_type=jnp.float32
    )
    out = (accum / total[..., None]).transpose(1, 0, 2)
    return out.reshape(tok, heads * HEAD_WIDTH).astype(jnp.bfloat16)


def project(heads_out, out_proj):
    tok = heads_out.shape[0]
    weight = lax.all_gather(out_proj, ("yl", "z"), axis=1, tiled=True)
    width = weight.shape[1]
    rows = tok // (NYH * NC)
    spread = jnp.broadcast_to(heads_out[None], (NX,) + heads_out.shape)
    all_x = lax.all_to_all(spread, "x", split_axis=0, concat_axis=0, tiled=True)
    part = jnp.dot(
        all_x.reshape(NX * tok, -1), weight, preferred_element_type=jnp.float32
    ).astype(jnp.bfloat16)
    part = part.reshape(NX, NYH, NC, rows, width)
    c, yh = lax.axis_index("c"), lax.axis_index("yh")
    got = lax.ppermute(lax.dynamic_index_in_dim(part, 1 - c, 2, False), "c", SWAP)
    part = add(lax.dynamic_index_in_dim(part, c, 2, False), got)
    got = lax.ppermute(lax.dynamic_index_in_dim(part, 1 - yh, 1, False), "yh", SWAP)
    part = add(lax.dynamic_index_in_dim(part, yh, 1, False), got)
    columns = lax.all_to_all(part, "x", split_axis=0, concat_axis=0, tiled=True)
    return columns.transpose(1, 0, 2).reshape(rows, NX * width)


def expert_part(rows, w_gate, w_up, w_down):
    gate_val = jnp.dot(rows, w_gate, preferred_element_type=jnp.float32)
    up_val = jnp.dot(rows, w_up, preferred_element_type=jnp.float32)
    hidden = (jax.nn.silu(gate_val) * up_val).astype(jnp.bfloat16)
    return jnp.dot(hidden, w_down, preferred_element_type=jnp.float32).astype(jnp.bfloat16)


def spread_z(own):
    cut = own.shape[0] // 16 * 8
    below = lax.ppermute(own, "z", UP)
    above = lax.ppermute(own, "z", DOWN)
    far_first = lax.ppermute(below[:cut], "z", UP)
    far_second = lax.ppermute(above[cut:], "z", DOWN)
    return own, below, above, jnp.concatenate([far_first, far_second], axis=0)


def collect_z(own, below, above, far):
    cut = own.shape[0] // 16 * 8
    from_above = lax.ppermute(far[:cut], "z", DOWN)
    from_below = lax.ppermute(far[cut:], "z", UP)
    below = jnp.concatenate([add(below[:cut], from_above), below[cut:]], axis=0)
    above = jnp.concatenate([above[:cut], add(above[cut:], from_below)], axis=0)
    return add(own, lax.ppermute(below, "z", DOWN), lax.ppermute(above, "z", UP))


def per_device(
    stream_in,
    queries,
    rotated_key_heads,
    values,
    doc_ids,
    out_proj,
    norm_gain,
    router,
    w_gate,
    w_up,
    w_down,
    routes,
):
    heads_out = attention(queries, rotated_key_heads, values, doc_ids)
    summed = project(heads_out, out_proj)
    resid = stream_in.astype(jnp.float32) + summed.astype(jnp.float32)
    width = resid.shape[1]
    normed = (
        resid * lax.rsqrt(jnp.mean(resid * resid, axis=1, keepdims=True) + 1e-05) * norm_gain
    ).astype(jnp.bfloat16)
    logits = jnp.dot(normed.astype(jnp.float32), router, precision=lax.Precision.HIGHEST)
    experts = router.shape[1]
    rows = normed.shape[0]
    cap = rows * 9 // 32
    slots = experts * cap
    hits = routes[:, :, None] == jnp.arange(experts, dtype=jnp.int32)
    flat_hits = hits.astype(jnp.int32).reshape(rows * 2, experts)
    before = jnp.cumsum(flat_hits, axis=0) - flat_hits
    slot = jnp.sum(before.reshape(rows, 2, experts) * hits.astype(jnp.int32), axis=-1)
    target = routes * cap + slot
    placed = target[:, :, None] == jnp.arange(slots, dtype=jnp.int32)[None, None, :]
    chooser = jnp.any(placed, axis=1).astype(jnp.bfloat16).T
    pair_logits = jnp.sum(jnp.where(hits, logits[:, None, :], 0.0), axis=-1)
    first_gate = 1.0 / (1.0 + jnp.exp(pair_logits[:, 1] - pair_logits[:, 0]))
    second_gate = 1.0 / (1.0 + jnp.exp(pair_logits[:, 0] - pair_logits[:, 1]))
    gate_pair = jnp.stack([first_gate, second_gate], axis=1)
    combiner = jnp.sum(jnp.where(placed, gate_pair[:, :, None], 0.0), axis=1)

    packed = jnp.dot(chooser, normed, preferred_element_type=jnp.float32).astype(jnp.bfloat16)
    arrived = lax.all_to_all(
        packed.reshape(experts, cap, width), ("x", "yl"), split_axis=0, concat_axis=0, tiled=True
    ).reshape(slots, width)
    over = lax.ppermute(arrived, "yh", SWAP)
    blocks = spread_z(arrived) + spread_z(over)
    sent = []
    for block in blocks:
        both = jnp.concatenate([block, lax.ppermute(block, "c", SWAP)], axis=0)
        out = expert_part(both, w_gate, w_up, w_down)
        sent.append(add(out[:slots], lax.ppermute(out[slots:], "c", SWAP)))
    home = add(collect_z(*sent[:4]), lax.ppermute(collect_z(*sent[4:]), "yh", SWAP))
    returned = lax.all_to_all(
        home.reshape(experts, cap, width), ("x", "yl"), split_axis=0, concat_axis=0, tiled=True
    ).reshape(slots, width)
    mixture = jnp.dot(combiner, returned.astype(jnp.float32), precision=lax.Precision.HIGHEST)
    return (resid + mixture).astype(jnp.bfloat16)


def solution(mesh):
    fine = Mesh(mesh.devices.reshape(NX, NYL, NZ, NYH, NC), ("x", "yl", "z", "yh", "c"))
    ctx, tp = ("x", "yl", "z"), ("yh", "c")
    placed = (
        P(ctx + tp, None),
        P(ctx, tp),
        P(ctx, tp),
        P(ctx, tp),
        P(ctx),
        P(tp, ctx),
        P(),
        P(),
        P(None, ctx + tp),
        P(None, ctx + tp),
        P(ctx + tp, None),
        P(ctx + tp, None),
    )
    return jax.shard_map(
        per_device, mesh=fine, in_specs=placed, out_specs=P(ctx + tp, None), check_vma=False
    )
```

time: 1140 us -> 482 us (0.42)
  the two profiles are of different devices: /device:TPU:1 before, /device:TPU:96 now
where the time goes in v1:
time: 482 us; the launch traced here: 473 us
  waiting for transfers between devices  178 us (37%)
  matrix products  120 us (25%)
  local copies, waits for them, and re-layouts  60.3 us (13%)
  starting transfers between devices  54.4 us (11%)
  blocking collectives  23 us (5%)
  other arithmetic  21.7 us (5%)
  between operations  14.7 us (3%)
    dot_general x8, matrix products, expert_part(): jnp.dot(hidden, w_down, preferred_element_type=jnp.float32)  66.7 us
    dot_general x8, matrix products, expert_part(): gate_val = jnp.dot(rows, w_gate, preferred_element_type=jnp.float32)  35.9 us
    ppermute x2, waiting for transfers between devices, collect_z(): from_above = lax.ppermute(far[:cut], 'z', DOWN)  23.1 us
    all_to_all x1, blocking collectives, per_device(): lax.all_to_all(packed.reshape(experts, cap, width), ('x', 'yl'), split_ax...  23 us
    unnamed x76, local copies, waits for them, and re-layouts  22.2 us
    ppermute x2, waiting for transfers between devices, collect_z(): lax.ppermute(below, 'z', DOWN)  20.5 us
    all_to_all x1, waiting for transfers between devices, per_device(): lax.all_to_all(home.reshape(experts, cap, width), ('x', 'yl'), split_axis...  19.5 us
    ppermute x1, waiting for transfers between devices, gather_keys(): below = lax.ppermute(here, 'z', UP)  17.5 us
  transfers between devices with their start and end apart: 47, of which 20 were waited for; matrix products, arithmetic and copies ran while one was open for 38% of the time, Pallas kernels for 0%

profile of v1, /device:TPU:96, one launch (start us, length us, event | category | flops | bytes accessed | tf_op | source)
XLA Modules:
  0.0 472.6 jit_solution(15681396730230369007)
XLA Ops:
  9.6 3.4 collective-permute-start
  13.0 4.6 collective-permute-start.1
  21.3 4.2 collective-permute-done.2
  25.6 2.0 collective-permute-start.4
  28.6 17.5 %collective-permute-done.3 = bf16[1632,128]{1,0:T(8,128)(2,1)S(1)} collective-permute-done((bf16[1632,128]{1,0:T(8,128)(2,1)S(1)}, bf16[1632,128]{1,0:T(8,128)(2,1)S(1)}, u32[]{:S(2)}, u32[]{:S(2)}) %collective-permute-start.3) | collective-permute-done | bytes 417824 | tf_op jit(solution)/shard_map/ppermute | solution.py:31
  46.1 2.0 collective-permute-start.5
  49.9 7.0 %collective-permute-done.5 = bf16[816,128]{1,0:T(8,128)(2,1)S(1)} collective-permute-done((bf16[816,128]{1,0:T(8,128)(2,1)S(1)}, bf16[816,128]{1,0:T(8,128)(2,1)S(1)}, u32[]{:S(2)}, u32[]{:S(2)}) %collective-permute-start.5) | collective-permute-done | bytes 208928 | tf_op jit(solution)/shard_map/ppermute | solution.py:34
  56.9 6.3 %collective-permute-done.6 = bf16[816,128]{1,0:T(8,128)(2,1)S(1)} collective-permute-done((bf16[816,128]{1,0:T(8,128)(2,1)S(1)}, bf16[816,128]{1,0:T(8,128)(2,1)S(1)}, u32[]{:S(2)}, u32[]{:S(2)}) %collective-permute-start.6) | collective-permute-done | bytes 208928 | tf_op jit(solution)/shard_map/ppermute | solution.py:35
  63.5 1.9 compare_and_fusion
  65.4 7.1 %fusion.48 = (f32[6,128]{1,0:T(8,128)S(1)}, bf16[6,128,3072]{1,2,0:T(8,128)(2,1)}) fusion(pred[128,3072]{0,1:T(8,128)(4,1)S(1)} %compare_and_fusion, bf16[3072,128,1]{1,0,2:T(8,128)(2,1)S(1)} %bitcast.116, bf16[128,6,128]{0,2,1:T(8,128)(2,1)} %bitcast.117), kind=kOutput, calls=%fused_computation.154 | convolution fusion | flops 1224477696 | bytes 6097920 | tf_op jit(solution)/shard_map/sub | solution.py:64
  72.5 3.2 fusion.20
  76.8 3.5 all-to-all-start
  80.3 11.6 %all-to-all-done = bf16[4,128,768]{2,1,0:T(8,128)(2,1)S(1)} async-done(((bf16[4,128,768]{2,1,0:T(8,128)(2,1)}), bf16[4,128,768]{2,1,0:T(8,128)(2,1)S(1)}, u32[]{:S(2)}, u32[]{:S(2)}) %all-to-all-start) | async-done | bytes 786464 | tf_op jit(solution)/shard_map/all_to_all | solution.py:79
  91.9 3.1 convolution_convert_fusion.9
  95.2 2.3 collective-permute-done.7
  97.7 3.6 collective-permute-start.8
  102.0 8.7 %collective-permute-done.8 = bf16[4,32,1536]{2,1,0:T(8,128)(2,1)S(1)} collective-permute-done((bf16[4,32,1536]{2,1,0:T(8,128)(2,1)S(1)}, bf16[4,32,1536]{2,1,0:T(8,128)(2,1)S(1)}, u32[]{:S(2)}, u32[]{:S(2)}) %collective-permute-start.8) | collective-permute-done | bytes 393248 | tf_op jit(solution)/shard_map/ppermute | solution.py:87
  111.6 4.1 all-to-all-start.1
  115.7 8.0 %all-to-all-done.1 = bf16[4,32,1536]{2,1,0:T(8,128)(2,1)S(1)} async-done(((bf16[4,32,1536]{2,1,0:T(8,128)(2,1)}), bf16[4,32,1536]{2,1,0:T(8,128)(2,1)S(1)}, u32[]{:S(2)}, u32[]{:S(2)}) %all-to-all-start.1) | async-done | bytes 393248 | tf_op jit(solution)/shard_map/all_to_all | solution.py:89
  127.3 23.0 %all_to_all.20 = bf16[8,9,6144]{2,1,0:T(8,128)(2,1)} all-to-all(bf16[8,9,6144]{2,1,0:T(8,128)(2,1)S(1)} %reshape.166), channel_id=1, replica_groups=mesh['x'=4,'yl'=2,'z'=4,'yh'=2,'c'=2] {'x','yl'}, dimensions={0} | all-to-all | bytes 1769472 | tf_op jit(solution)/shard_map/all_to_all | solution.py:158
  150.3 2.7 reshape.167
  153.0 2.0 collective-permute-start.15
  155.0 2.6 collective-permute-start.25
  158.9 13.0 %collective-permute-done.11 = bf16[72,6144]{1,0:T(8,128)(2,1)} collective-permute-done((bf16[72,6144]{1,0:T(8,128)(2,1)}, bf16[72,6144]{1,0:T(8,128)(2,1)}, u32[]{:S(2)}, u32[]{:S(2)}) %collective-permute-start.11) | collective-permute-done | bytes 884768 | tf_op jit(solution)/shard_map/ppermute | solution.py:102
  177.6 4.6 fusion.66
  182.1 8.1 %convolution_convert_fusion.7 = bf16[144,6144]{1,0:T(8,128)(2,1)} fusion(bf16[512,6144]{1,0:T(8,128)(2,1)} %param.23, f32[144,512]{1,0:T(8,128)} %fusion.66, bf16[144,6144]{1,0:T(8,128)(2,1)S(1)} %constant_dynamic-update-slice_fusion.21, bf16[6144,512]{1,0:T(8,128)(2,1)} %param.22), kind=kOutput, calls=%fused_computation.14 | convolution fusion | flops 1813266432 | bytes 16416768 | tf_op jit(solution)/shard_map/dot_general | solution.py:97
  190.2 2.2 slice.164
  192.4 2.7 collective-permute-start.28
  196.4 2.2 constant_dynamic-update-slice_fusion.29
  204.0 2.2 pad_maximum_fusion
  206.5 5.2 %fusion.70 = f32[144,512]{1,0:T(8,128)} fusion(bf16[144,6144]{1,0:T(8,128)(2,1)S(1)} %constant_dynamic-update-slice_fusion.30, bf16[6144,512]{1,0:T(8,128)(2,1)} %param.21), kind=kOutput, calls=%fused_computation.168 | convolution fusion | flops 905969664 | bytes 8355840 | tf_op jit(solution)/shard_map/dot_general | solution.py:94
  211.7 3.3 collective-permute-done.28
  218.3 2.3 collective-permute-start.31
  221.4 8.6 %convolution_convert_fusion.3 = bf16[144,6144]{1,0:T(8,128)(2,1)} fusion(bf16[512,6144]{1,0:T(8,128)(2,1)} %param.23, f32[144,512]{1,0:T(8,128)} %fusion.70, bf16[144,6144]{1,0:T(8,128)(2,1)} %copy-done.3, bf16[6144,512]{1,0:T(8,128)(2,1)} %param.22), kind=kOutput, calls=%fused_computation.10 | convolution fusion | flops 1813266432 | bytes 16416768 | tf_op jit(solution)/shard_map/dot_general | solution.py:97
  229.9 2.1 constant_dynamic-update-slice_fusion.28
  232.1 5.3 %fusion.69 = f32[144,512]{1,0:T(8,128)} fusion(bf16[144,6144]{1,0:T(8,128)(2,1)} %constant_dynamic-update-slice_fusion.28, bf16[6144,512]{1,0:T(8,128)(2,1)} %param.21), kind=kOutput, calls=%fused_computation.167 | convolution fusion | flops 905969664 | bytes 8355840 | tf_op jit(solution)/shard_map/dot_general | solution.py:94
  238.3 8.6 %convolution_convert_fusion.4 = bf16[144,6144]{1,0:T(8,128)(2,1)} fusion(bf16[512,6144]{1,0:T(8,128)(2,1)} %param.23, f32[144,512]{1,0:T(8,128)} %fusion.69, bf16[144,6144]{1,0:T(8,128)(2,1)} %constant_dynamic-update-slice_fusion.28, bf16[6144,512]{1,0:T(8,128)(2,1)} %param.22), kind=kOutput, calls=%fused_computation.11 | convolution fusion | flops 1813266432 | bytes 16416768 | tf_op jit(solution)/shard_map/dot_general | solution.py:97
  248.3 4.6 fusion.67
  252.9 8.1 %convolution_convert_fusion.6 = bf16[144,6144]{1,0:T(8,128)(2,1)} fusion(bf16[512,6144]{1,0:T(8,128)(2,1)} %param.23, f32[144,512]{1,0:T(8,128)} %fusion.67, bf16[144,6144]{1,0:T(8,128)(2,1)S(1)} %constant_dynamic-update-slice_fusion.23, bf16[6144,512]{1,0:T(8,128)(2,1)} %param.22), kind=kOutput, calls=%fused_computation.13 | convolution fusion | flops 1813266432 | bytes 16416768 | tf_op jit(solution)/shard_map/dot_general | solution.py:97
  261.0 2.3 constant_dynamic-update-slice_fusion.38
  268.9 2.2 constant_dynamic-update-slice_fusion.25
  271.1 5.1 %fusion.68 = f32[144,512]{1,0:T(8,128)} fusion(bf16[144,6144]{1,0:T(8,128)(2,1)} %constant_dynamic-update-slice_fusion.25, bf16[6144,512]{1,0:T(8,128)(2,1)} %param.21), kind=kOutput, calls=%fused_computation.166 | convolution fusion | flops 905969664 | bytes 8355840 | tf_op jit(solution)/shard_map/dot_general | solution.py:94
  276.2 8.7 %convolution_convert_fusion.5 = bf16[144,6144]{1,0:T(8,128)(2,1)} fusion(bf16[512,6144]{1,0:T(8,128)(2,1)} %param.23, f32[144,512]{1,0:T(8,128)} %fusion.68, bf16[144,6144]{1,0:T(8,128)(2,1)} %constant_dynamic-update-slice_fusion.25, bf16[6144,512]{1,0:T(8,128)(2,1)} %param.22), kind=kOutput, calls=%fused_computation.12 | convolution fusion | flops 1813266432 | bytes 16416768 | tf_op jit(solution)/shard_map/dot_general | solution.py:97
  287.3 2.3 slice.171
  289.6 2.1 pad_maximum_fusion.3
  293.4 4.6 fusion.73
  297.9 8.6 %convolution_convert_fusion = bf16[144,6144]{1,0:T(8,128)(2,1)} fusion(bf16[512,6144]{1,0:T(8,128)(2,1)} %param.23, f32[144,512]{1,0:T(8,128)} %fusion.73, bf16[144,6144]{1,0:T(8,128)(2,1)} %copy-done.2, bf16[6144,512]{1,0:T(8,128)(2,1)} %param.22), kind=kOutput, calls=%fused_computation.7 | convolution fusion | flops 1813266432 | bytes 16416768 | tf_op jit(solution)/shard_map/dot_general | solution.py:97
  308.0 4.7 fusion.71
  313.7 8.2 %convolution_convert_fusion.2 = bf16[144,6144]{1,0:T(8,128)(2,1)} fusion(bf16[512,6144]{1,0:T(8,128)(2,1)} %param.23, f32[144,512]{1,0:T(8,128)} %fusion.71, bf16[144,6144]{1,0:T(8,128)(2,1)S(1)} %constant_dynamic-update-slice_fusion.32, bf16[6144,512]{1,0:T(8,128)(2,1)} %param.22), kind=kOutput, calls=%fused_computation.9 | convolution fusion | flops 1813266432 | bytes 16416768 | tf_op jit(solution)/shard_map/dot_general | solution.py:97
  321.9 2.3 slice.182
  326.5 2.1 add_convert_fusion.9
  335.1 8.1 %convolution_convert_fusion.1 = bf16[144,6144]{1,0:T(8,128)(2,1)} fusion(bf16[512,6144]{1,0:T(8,128)(2,1)} %param.23, f32[144,512]{1,0:T(8,128)} %fusion.72, bf16[144,6144]{1,0:T(8,128)(2,1)S(1)} %constant_dynamic-update-slice_fusion.34, bf16[6144,512]{1,0:T(8,128)(2,1)} %param.22), kind=kOutput, calls=%fused_computation.8 | convolution fusion | flops 1813266432 | bytes 16416768 | tf_op jit(solution)/shard_map/dot_general | solution.py:97
  344.8 3.1 collective-permute-start.23
  351.0 10.7 %collective-permute-done.19 = bf16[32,6144]{1,0:T(8,128)(2,1)S(1)} collective-permute-done((bf16[32,6144]{1,0:T(8,128)(2,1)S(1)}, bf16[32,6144]{1,0:T(8,128)(2,1)S(1)}, u32[]{:S(2)}, u32[]{:S(2)}) %collective-permute-start.19) | collective-permute-done | bytes 393248 | tf_op jit(solution)/shard_map/ppermute | solution.py:111
  363.1 12.4 %collective-permute-done.36 = bf16[32,6144]{1,0:T(8,128)(2,1)S(1)} collective-permute-done((bf16[32,6144]{1,0:T(8,128)(2,1)S(1)}, bf16[32,6144]{1,0:T(8,128)(2,1)S(1)}, u32[]{:S(2)}, u32[]{:S(2)}) %collective-permute-start.36) | collective-permute-done | bytes 393248 | tf_op jit(solution)/shard_map/ppermute | solution.py:111
  375.6 10.9 %collective-permute-done.40 = bf16[40,6144]{1,0:T(8,128)(2,1)S(1)} collective-permute-done((bf16[40,6144]{1,0:T(8,128)(2,1)S(1)}, bf16[40,6144]{1,0:T(8,128)(2,1)S(1)}, u32[]{:S(2)}, u32[]{:S(2)}) %collective-permute-start.40) | collective-permute-done | bytes 491552 | tf_op jit(solution)/shard_map/ppermute | solution.py:112
  386.8 3.3 collective-permute-start.41
  391.0 20.5 %collective-permute-done.37 = bf16[72,6144]{1,0:T(8,128)(2,1)S(1)} collective-permute-done((bf16[72,6144]{1,0:T(8,128)(2,1)S(1)}, bf16[72,6144]{1,0:T(8,128)(2,1)S(1)}, u32[]{:S(2)}, u32[]{:S(2)}) %collective-permute-start.37) | collective-permute-done | bytes 884768 | tf_op jit(solution)/shard_map/ppermute | solution.py:115
  413.1 2.8 collective-permute-start.42
  415.9 7.0 %collective-permute-done.24 = bf16[72,6144]{1,0:T(8,128)(2,1)S(1)} collective-permute-done((bf16[72,6144]{1,0:T(8,128)(2,1)S(1)}, bf16[72,6144]{1,0:T(8,128)(2,1)S(1)}, u32[]{:S(2)}, u32[]{:S(2)}) %collective-permute-start.24) | collective-permute-done | bytes 884768 | tf_op jit(solution)/shard_map/ppermute | solution.py:115
  422.9 11.6 %collective-permute-done.42 = bf16[72,6144]{1,0:T(8,128)(2,1)S(1)} collective-permute-done((bf16[72,6144]{1,0:T(8,128)(2,1)S(1)}, bf16[72,6144]{1,0:T(8,128)(2,1)S(1)}, u32[]{:S(2)}, u32[]{:S(2)}) %collective-permute-start.42) | collective-permute-done | bytes 884768 | tf_op jit(solution)/shard_map/ppermute | solution.py:168
  437.9 3.6 all-to-all-start.3
  442.0 19.5 %all-to-all-done.3 = bf16[8,9,6144]{2,1,0:T(8,128)(2,1)S(1)} async-done(((bf16[8,9,6144]{2,1,0:T(8,128)(2,1)}), bf16[8,9,6144]{2,1,0:T(8,128)(2,1)S(1)}, u32[]{:S(2)}, u32[]{:S(2)}) %all-to-all-start.3) | async-done | bytes 884768 | tf_op jit(solution)/shard_map/all_to_all | solution.py:169
  462.9 2.5 fusion.5
  (224 shorter events, 71.9 us)
Async XLA Ops:
  6.5 434.9 %copy-start = (f32[6144,8]{0,1:T(8,128)S(1)}, f32[6144,8]{0,1:T(8,128)}, u32[]{:S(2)}) copy-start(f32[6144,8]{0,1:T(8,128)} %param.20) | copy-start | bytes 589828
  6.5 21.2 %copy-start.22 = (bf16[128,768]{1,0:T(8,128)(2,1)S(1)}, bf16[128,768]{1,0:T(8,128)(2,1)}, u32[]{:S(2)}) copy-start(bf16[128,768]{1,0:T(8,128)(2,1)} %param.14) | copy-start | bytes 589828
  6.5 85.3 %all-gather.2.cloned.1.call-start = ((), (), s32[]{:S(2)}) async-start(), calls=%async_computation.4 | async-start | bytes 2654208 | tf_op jit(solution)/shard_map/all_gather | solution.py:75
  9.6 8.9 %collective-permute-start = (bf16[272,128]{1,0:T(8,128)(2,1)S(1)}, bf16[272,128]{1,0:T(8,128)(2,1)S(1)}, u32[]{:S(2)}, u32[]{:S(2)}) collective-permute-start(bf16[272,128]{1,0:T(8,128)(2,1)S(1)} %pad_maximum_fusion.6), channel_id=1, source_target_pairs={{0,32},{32,64},{64,96},{1,33},{33,65},{65,97},{2,34},{34,66},{66,9... | collective-permute-start | bytes 208904 | tf_op jit(solution)/shard_map/ppermute | solution.py:26
  13.0 6.6 %collective-permute-start.1 = (bf16[272,128]{1,0:T(8,128)(2,1)S(1)}, bf16[272,128]{1,0:T(8,128)(2,1)S(1)}, u32[]{:S(2)}, u32[]{:S(2)}) collective-permute-start(bf16[272,128]{1,0:T(8,128)(2,1)S(1)} %pad_maximum_fusion.6), channel_id=1, source_target_pairs={{0,64},{32,96},{1,65},{33,97},{2,66},{34,98},{3,67},{35,99},{4,68}... | collective-permute-start | bytes 208904 | tf_op jit(solution)/shard_map/ppermute | solution.py:27
  19.6 5.9 %collective-permute-start.2 = (bf16[816,128]{1,0:T(8,128)(2,1)S(1)}, bf16[816,128]{1,0:T(8,128)(2,1)S(1)}, u32[]{:S(2)}, u32[]{:S(2)}) collective-permute-start(bf16[816,128]{1,0:T(8,128)(2,1)S(1)} %get-tuple-element.11), channel_id=1, source_target_pairs={{0,16},{16,0},{1,17},{17,1},{2,18},{18,2},{3,19},{19,3},{4,20},{20... | collective-permute-start | bytes 626696 | tf_op jit(solution)/shard_map/ppermute | solution.py:29
  25.6 20.5 %collective-permute-start.3 = (bf16[1632,128]{1,0:T(8,128)(2,1)S(1)}, bf16[1632,128]{1,0:T(8,128)(2,1)S(1)}, u32[]{:S(2)}, u32[]{:S(2)}) collective-permute-start(bf16[1632,128]{1,0:T(8,128)(2,1)S(1)} %get-tuple-element.7), channel_id=1, source_target_pairs={{0,4},{4,8},{8,12},{12,0},{1,5},{5,9},{9,13},{13,1},{2,6},{6,10},{... | collective-permute-start | bytes 1253384 | tf_op jit(solution)/shard_map/ppermute | solution.py:31
  25.6 24.0 %collective-permute-start.4 = (bf16[1632,128]{1,0:T(8,128)(2,1)S(1)}, bf16[1632,128]{1,0:T(8,128)(2,1)S(1)}, u32[]{:S(2)}, u32[]{:S(2)}) collective-permute-start(bf16[1632,128]{1,0:T(8,128)(2,1)S(1)} %get-tuple-element.7), channel_id=1, source_target_pairs={{4,0},{8,4},{12,8},{0,12},{5,1},{9,5},{13,9},{1,13},{6,2},{10,6},{... | collective-permute-start | bytes 1253384 | tf_op jit(solution)/shard_map/ppermute | solution.py:32
  46.1 10.8 %collective-permute-start.5 = (bf16[816,128]{1,0:T(8,128)(2,1)S(1)}, bf16[816,128]{1,0:T(8,128)(2,1)S(1)}, u32[]{:S(2)}, u32[]{:S(2)}) collective-permute-start(bf16[816,128]{1,0:T(8,128)(2,1)S(1)} %slice.158), channel_id=1, source_target_pairs={{0,4},{4,8},{8,12},{12,0},{1,5},{5,9},{9,13},{13,1},{2,6},{6,10},{... | collective-permute-start | bytes 626696 | tf_op jit(solution)/shard_map/ppermute | solution.py:34
  49.7 13.6 %collective-permute-start.6 = (bf16[816,128]{1,0:T(8,128)(2,1)S(1)}, bf16[816,128]{1,0:T(8,128)(2,1)S(1)}, u32[]{:S(2)}, u32[]{:S(2)}) collective-permute-start(bf16[816,128]{1,0:T(8,128)(2,1)S(1)} %slice.159), channel_id=1, source_target_pairs={{4,0},{8,4},{12,8},{0,12},{5,1},{9,5},{13,9},{1,13},{6,2},{10,6},{... | collective-permute-start | bytes 626696 | tf_op jit(solution)/shard_map/ppermute | solution.py:35
  56.9 6.6 %copy-start.25 = (s32[128]{0:T(128)S(1)}, s32[128]{0:T(128)}, u32[]{:S(2)}) copy-start(s32[128]{0:T(128)} %param.17) | copy-start | bytes 1540
  76.8 15.1 %all-to-all-start = ((bf16[4,128,768]{2,1,0:T(8,128)(2,1)}), bf16[4,128,768]{2,1,0:T(8,128)(2,1)S(1)}, u32[]{:S(2)}, u32[]{:S(2)}) async-start(bf16[4,128,768]{2,1,0:T(8,128)(2,1)} %broadcast_in_dim.81), calls=%async_computation | async-start | bytes 1572864 | tf_op jit(solution)/shard_map/all_to_all | solution.py:79
  95.0 6.3 %copy-start.24 = (s32[32,2]{0,1:T(2,128)S(1)}, s32[32,2]{0,1:T(2,128)}, u32[]{:S(2)}) copy-start(s32[32,2]{0,1:T(2,128)} %param.24) | copy-start | bytes 772
  95.1 2.4 collective-permute-start.7
  97.7 13.0 %collective-permute-start.8 = (bf16[4,32,1536]{2,1,0:T(8,128)(2,1)S(1)}, bf16[4,32,1536]{2,1,0:T(8,128)(2,1)S(1)}, u32[]{:S(2)}, u32[]{:S(2)}) collective-permute-start(bf16[4,32,1536]{2,1,0:T(8,128)(2,1)S(1)} %dynamic-slice_bitcast_fusion.1), channel_id=1, source_target_pairs={{0,2},{2,0},{1,3},{3,1},{4,6},{6,4},{5,7},{7,5},{8,10},{10,8},{9,1... | collective-permute-start | bytes 1179656 | tf_op jit(solution)/shard_map/ppermute | solution.py:87
  111.6 12.3 %copy-start.15 = (bf16[32,6144]{1,0:T(8,128)(2,1)S(1)}, bf16[32,6144]{1,0:T(8,128)(2,1)}, u32[]{:S(2)}) copy-start(bf16[32,6144]{1,0:T(8,128)(2,1)} %param.13) | copy-start | bytes 1179652
  111.6 12.2 %all-to-all-start.1 = ((bf16[4,32,1536]{2,1,0:T(8,128)(2,1)}), bf16[4,32,1536]{2,1,0:T(8,128)(2,1)S(1)}, u32[]{:S(2)}, u32[]{:S(2)}) async-start(bf16[4,32,1536]{2,1,0:T(8,128)(2,1)} %fusion.23), calls=%async_computation.1 | async-start | bytes 786432 | tf_op jit(solution)/shard_map/all_to_all | solution.py:89
  115.7 8.4 %copy-start.23 = (f32[6144]{0:T(1024)S(1)}, f32[6144]{0:T(1024)}, u32[]{:S(2)}) copy-start(f32[6144]{0:T(1024)} %param.19) | copy-start | bytes 73732
  153.0 18.8 %collective-permute-start.11 = (bf16[72,6144]{1,0:T(8,128)(2,1)}, bf16[72,6144]{1,0:T(8,128)(2,1)}, u32[]{:S(2)}, u32[]{:S(2)}) collective-permute-start(bf16[72,6144]{1,0:T(8,128)(2,1)} %reshape.167), channel_id=1, source_target_pairs={{0,4},{4,8},{8,12},{12,0},{1,5},{5,9},{9,13},{13,1},{2,6},{6,10},{... | collective-permute-start | bytes 2654216 | tf_op jit(solution)/shard_map/ppermute | solution.py:102
  153.0 22.1 %collective-permute-start.15 = (bf16[72,6144]{1,0:T(8,128)(2,1)}, bf16[72,6144]{1,0:T(8,128)(2,1)}, u32[]{:S(2)}, u32[]{:S(2)}) collective-permute-start(bf16[72,6144]{1,0:T(8,128)(2,1)} %reshape.167), channel_id=1, source_target_pairs={{4,0},{8,4},{12,8},{0,12},{5,1},{9,5},{13,9},{1,13},{6,2},{10,6},{... | collective-permute-start | bytes 2654216 | tf_op jit(solution)/shard_map/ppermute | solution.py:103
  155.0 22.5 %collective-permute-start.9 = (bf16[72,6144]{1,0:T(8,128)(2,1)}, bf16[72,6144]{1,0:T(8,128)(2,1)S(1)}, u32[]{:S(2)}, u32[]{:S(2)}) collective-permute-start(bf16[72,6144]{1,0:T(8,128)(2,1)} %reshape.167), channel_id=1, source_target_pairs={{0,1},{1,0},{2,3},{3,2},{4,5},{5,4},{6,7},{7,6},{8,9},{9,8},{10,11... | collective-permute-start | bytes 2654216 | tf_op jit(solution)/shard_map/ppermute | solution.py:165
  155.0 37.3 %collective-permute-start.25 = (bf16[72,6144]{1,0:T(8,128)(2,1)}, bf16[72,6144]{1,0:T(8,128)(2,1)}, u32[]{:S(2)}, u32[]{:S(2)}) collective-permute-start(bf16[72,6144]{1,0:T(8,128)(2,1)} %reshape.167), channel_id=1, source_target_pairs={{0,2},{2,0},{1,3},{3,1},{4,6},{6,4},{5,7},{7,5},{8,10},{10,8},{9,1... | collective-permute-start | bytes 2654216 | tf_op jit(solution)/shard_map/ppermute | solution.py:161
  173.6 26.2 %collective-permute-start.14 = (bf16[32,6144]{1,0:T(8,128)(2,1)}, bf16[32,6144]{1,0:T(8,128)(2,1)}, u32[]{:S(2)}, u32[]{:S(2)}) collective-permute-start(bf16[32,6144]{1,0:T(8,128)(2,1)} %slice.168), channel_id=1, source_target_pairs={{0,4},{4,8},{8,12},{12,0},{1,5},{5,9},{9,13},{13,1},{2,6},{6,10},{... | collective-permute-start | bytes 1179656 | tf_op jit(solution)/shard_map/ppermute | solution.py:104
  176.9 24.9 %collective-permute-start.16 = (bf16[40,6144]{1,0:T(8,128)(2,1)}, bf16[40,6144]{1,0:T(8,128)(2,1)}, u32[]{:S(2)}, u32[]{:S(2)}) collective-permute-start(bf16[40,6144]{1,0:T(8,128)(2,1)} %slice.169), channel_id=1, source_target_pairs={{4,0},{8,4},{12,8},{0,12},{5,1},{9,5},{13,9},{1,13},{6,2},{10,6},{... | collective-permute-start | bytes 1474568 | tf_op jit(solution)/shard_map/ppermute | solution.py:105
  192.4 223.5 %collective-permute-start.10 = (bf16[72,6144]{1,0:T(8,128)(2,1)}, bf16[72,6144]{1,0:T(8,128)(2,1)}, u32[]{:S(2)}, u32[]{:S(2)}) collective-permute-start(bf16[72,6144]{1,0:T(8,128)(2,1)} %slice.164), channel_id=1, source_target_pairs={{0,1},{1,0},{2,3},{3,2},{4,5},{5,4},{6,7},{7,6},{8,9},{9,8},{10,11... | collective-permute-start | bytes 2654216 | tf_op jit(solution)/shard_map/ppermute | solution.py:167
  192.4 22.6 %collective-permute-start.28 = (bf16[72,6144]{1,0:T(8,128)(2,1)}, bf16[72,6144]{1,0:T(8,128)(2,1)}, u32[]{:S(2)}, u32[]{:S(2)}) collective-permute-start(bf16[72,6144]{1,0:T(8,128)(2,1)} %collective-permute-done.25), channel_id=1, source_target_pairs={{0,4},{4,8},{8,12},{12,0},{1,5},{5,9},{9,13},{13,1},{2,6},{6,10},{... | collective-permute-start | bytes 2654216 | tf_op jit(solution)/shard_map/ppermute | solution.py:102
  195.1 23.2 %collective-permute-start.32 = (bf16[72,6144]{1,0:T(8,128)(2,1)}, bf16[72,6144]{1,0:T(8,128)(2,1)S(1)}, u32[]{:S(2)}, u32[]{:S(2)}) collective-permute-start(bf16[72,6144]{1,0:T(8,128)(2,1)} %collective-permute-done.25), channel_id=1, source_target_pairs={{4,0},{8,4},{12,8},{0,12},{5,1},{9,5},{13,9},{1,13},{6,2},{10,6},{... | collective-permute-start | bytes 2654216 | tf_op jit(solution)/shard_map/ppermute | solution.py:103
  199.8 6.4 %collective-permute-start.26 = (bf16[72,6144]{1,0:T(8,128)(2,1)}, bf16[72,6144]{1,0:T(8,128)(2,1)S(1)}, u32[]{:S(2)}, u32[]{:S(2)}) collective-permute-start(bf16[72,6144]{1,0:T(8,128)(2,1)} %collective-permute-done.25), channel_id=1, source_target_pairs={{0,1},{1,0},{2,3},{3,2},{4,5},{5,4},{6,7},{7,6},{8,9},{9,8},{10,11... | collective-permute-start | bytes 2654216 | tf_op jit(solution)/shard_map/ppermute | solution.py:165
  201.9 28.1 %collective-permute-start.21 = (bf16[72,6144]{1,0:T(8,128)(2,1)}, bf16[72,6144]{1,0:T(8,128)(2,1)}, u32[]{:S(2)}, u32[]{:S(2)}) collective-permute-start(bf16[72,6144]{1,0:T(8,128)(2,1)} %collective-permute-done.15), channel_id=1, source_target_pairs={{0,1},{1,0},{2,3},{3,2},{4,5},{5,4},{6,7},{7,6},{8,9},{9,8},{10,11... | collective-permute-start | bytes 2654216 | tf_op jit(solution)/shard_map/ppermute | solution.py:165
  206.2 40.7 %collective-permute-start.12 = (bf16[72,6144]{1,0:T(8,128)(2,1)}, bf16[72,6144]{1,0:T(8,128)(2,1)}, u32[]{:S(2)}, u32[]{:S(2)}) collective-permute-start(bf16[72,6144]{1,0:T(8,128)(2,1)} %collective-permute-done.11), channel_id=1, source_target_pairs={{0,1},{1,0},{2,3},{3,2},{4,5},{5,4},{6,7},{7,6},{8,9},{9,8},{10,11... | collective-permute-start | bytes 2654216 | tf_op jit(solution)/shard_map/ppermute | solution.py:165
  206.5 5.2 %copy-start.3 = (bf16[144,6144]{1,0:T(8,128)(2,1)}, bf16[144,6144]{1,0:T(8,128)(2,1)S(1)}, u32[]{:S(2)}) copy-start(bf16[144,6144]{1,0:T(8,128)(2,1)S(1)} %constant_dynamic-update-slice_fusion.30) | copy-start | bytes 5308420
  215.0 53.7 %collective-permute-start.17 = (bf16[72,6144]{1,0:T(8,128)(2,1)}, bf16[72,6144]{1,0:T(8,128)(2,1)}, u32[]{:S(2)}, u32[]{:S(2)}) collective-permute-start(bf16[72,6144]{1,0:T(8,128)(2,1)} %pad_maximum_fusion), channel_id=1, source_target_pairs={{0,1},{1,0},{2,3},{3,2},{4,5},{5,4},{6,7},{7,6},{8,9},{9,8},{10,11... | collective-permute-start | bytes 2654216 | tf_op jit(solution)/shard_map/ppermute | solution.py:165
  218.3 48.3 %collective-permute-start.31 = (bf16[32,6144]{1,0:T(8,128)(2,1)}, bf16[32,6144]{1,0:T(8,128)(2,1)}, u32[]{:S(2)}, u32[]{:S(2)}) collective-permute-start(bf16[32,6144]{1,0:T(8,128)(2,1)} %slice.184), channel_id=1, source_target_pairs={{0,4},{4,8},{8,12},{12,0},{1,5},{5,9},{9,13},{13,1},{2,6},{6,10},{... | collective-permute-start | bytes 1179656 | tf_op jit(solution)/shard_map/ppermute | solution.py:104
  229.9 54.9 %collective-permute-start.33 = (bf16[40,6144]{1,0:T(8,128)(2,1)}, bf16[40,6144]{1,0:T(8,128)(2,1)}, u32[]{:S(2)}, u32[]{:S(2)}) collective-permute-start(bf16[40,6144]{1,0:T(8,128)(2,1)} %slice.185), channel_id=1, source_target_pairs={{4,0},{8,4},{12,8},{0,12},{5,1},{9,5},{13,9},{1,13},{6,2},{10,6},{... | collective-permute-start | bytes 1474568 | tf_op jit(solution)/shard_map/ppermute | solution.py:105
  232.1 5.3 %copy-start.13 = (bf16[144,6144]{1,0:T(8,128)(2,1)S(1)}, bf16[144,6144]{1,0:T(8,128)(2,1)}, u32[]{:S(2)}) copy-start(bf16[144,6144]{1,0:T(8,128)(2,1)} %convolution_convert_fusion.3) | copy-start | bytes 5308420
  246.9 143.4 %collective-permute-start.27 = (bf16[72,6144]{1,0:T(8,128)(2,1)}, bf16[72,6144]{1,0:T(8,128)(2,1)}, u32[]{:S(2)}, u32[]{:S(2)}) collective-permute-start(bf16[72,6144]{1,0:T(8,128)(2,1)} %slice.180), channel_id=1, source_target_pairs={{0,1},{1,0},{2,3},{3,2},{4,5},{5,4},{6,7},{7,6},{8,9},{9,8},{10,11... | collective-permute-start | bytes 2654216 | tf_op jit(solution)/shard_map/ppermute | solution.py:167
  266.6 57.6 %collective-permute-start.22 = (bf16[72,6144]{1,0:T(8,128)(2,1)}, bf16[72,6144]{1,0:T(8,128)(2,1)}, u32[]{:S(2)}, u32[]{:S(2)}) collective-permute-start(bf16[72,6144]{1,0:T(8,128)(2,1)} %slice.175), channel_id=1, source_target_pairs={{0,1},{1,0},{2,3},{3,2},{4,5},{5,4},{6,7},{7,6},{8,9},{9,8},{10,11... | collective-permute-start | bytes 2654216 | tf_op jit(solution)/shard_map/ppermute | solution.py:167
  268.7 57.4 %collective-permute-start.13 = (bf16[72,6144]{1,0:T(8,128)(2,1)}, bf16[72,6144]{1,0:T(8,128)(2,1)}, u32[]{:S(2)}, u32[]{:S(2)}) collective-permute-start(bf16[72,6144]{1,0:T(8,128)(2,1)} %slice.166), channel_id=1, source_target_pairs={{0,1},{1,0},{2,3},{3,2},{4,5},{5,4},{6,7},{7,6},{8,9},{9,8},{10,11... | collective-permute-start | bytes 2654216 | tf_op jit(solution)/shard_map/ppermute | solution.py:167
  284.9 6.9 %collective-permute-start.38 = (bf16[72,6144]{1,0:T(8,128)(2,1)}, bf16[72,6144]{1,0:T(8,128)(2,1)S(1)}, u32[]{:S(2)}, u32[]{:S(2)}) collective-permute-start(bf16[72,6144]{1,0:T(8,128)(2,1)} %copy-done.20), channel_id=1, source_target_pairs={{0,1},{1,0},{2,3},{3,2},{4,5},{5,4},{6,7},{7,6},{8,9},{9,8},{10,11... | collective-permute-start | bytes 2654216 | tf_op jit(solution)/shard_map/ppermute | solution.py:165
  291.7 14.8 %collective-permute-start.29 = (bf16[72,6144]{1,0:T(8,128)(2,1)}, bf16[72,6144]{1,0:T(8,128)(2,1)}, u32[]{:S(2)}, u32[]{:S(2)}) collective-permute-start(bf16[72,6144]{1,0:T(8,128)(2,1)} %collective-permute-done.28), channel_id=1, source_target_pairs={{0,1},{1,0},{2,3},{3,2},{4,5},{5,4},{6,7},{7,6},{8,9},{9,8},{10,11... | collective-permute-start | bytes 2654216 | tf_op jit(solution)/shard_map/ppermute | solution.py:165
  306.5 23.5 %collective-permute-start.34 = (bf16[72,6144]{1,0:T(8,128)(2,1)}, bf16[72,6144]{1,0:T(8,128)(2,1)}, u32[]{:S(2)}, u32[]{:S(2)}) collective-permute-start(bf16[72,6144]{1,0:T(8,128)(2,1)} %pad_maximum_fusion.3), channel_id=1, source_target_pairs={{0,1},{1,0},{2,3},{3,2},{4,5},{5,4},{6,7},{7,6},{8,9},{9,8},{10,11... | collective-permute-start | bytes 2654216 | tf_op jit(solution)/shard_map/ppermute | solution.py:165
  321.9 9.7 %slice-start = ((s8[6291456]{0:T(1024)(128)(4,1)}), s8[4194304]{0:T(1024)(128)(4,1)S(1)}, s32[]{:S(2)}) async-start(s8[6291456]{0:T(1024)(128)(4,1)} %bitcast.105), calls=%async_computation.5 | async-start | bytes 8388608
  324.2 4.4 collective-permute-start.18
  326.1 5.5 %slice-start.1 = ((s8[6291456]{0:T(1024)(128)(4,1)}), s8[2097152]{0:T(1024)(128)(4,1)S(1)}, s32[]{:S(2)}) async-start(s8[6291456]{0:T(1024)(128)(4,1)} %bitcast.105), calls=%async_computation.6 | async-start | bytes 4194304
  326.1 18.8 %collective-permute-start.39 = (bf16[72,6144]{1,0:T(8,128)(2,1)}, bf16[72,6144]{1,0:T(8,128)(2,1)}, u32[]{:S(2)}, u32[]{:S(2)}) collective-permute-start(bf16[72,6144]{1,0:T(8,128)(2,1)} %slice.191), channel_id=1, source_target_pairs={{0,1},{1,0},{2,3},{3,2},{4,5},{5,4},{6,7},{7,6},{8,9},{9,8},{10,11... | collective-permute-start | bytes 2654216 | tf_op jit(solution)/shard_map/ppermute | solution.py:167
  329.5 19.9 %collective-permute-start.30 = (bf16[72,6144]{1,0:T(8,128)(2,1)}, bf16[72,6144]{1,0:T(8,128)(2,1)}, u32[]{:S(2)}, u32[]{:S(2)}) collective-permute-start(bf16[72,6144]{1,0:T(8,128)(2,1)} %slice.182), channel_id=1, source_target_pairs={{0,1},{1,0},{2,3},{3,2},{4,5},{5,4},{6,7},{7,6},{8,9},{9,8},{10,11... | collective-permute-start | bytes 2654216 | tf_op jit(solution)/shard_map/ppermute | solution.py:167
  344.5 4.9 %copy-start.21 = (bf16[32,6144]{1,0:T(8,128)(2,1)S(1)}, bf16[32,6144]{1,0:T(8,128)(2,1)}, u32[]{:S(2)}) copy-start(bf16[32,6144]{1,0:T(8,128)(2,1)} %slice.172) | copy-start | bytes 1179652
  344.5 5.0 %copy-start.10 = (bf16[144,6144]{1,0:T(8,128)(2,1)S(1)}, bf16[144,6144]{1,0:T(8,128)(2,1)}, u32[]{:S(2)}) copy-start(bf16[144,6144]{1,0:T(8,128)(2,1)} %convolution_convert_fusion.2) | copy-start | bytes 5308420
  344.5 17.3 %collective-permute-start.35 = (bf16[72,6144]{1,0:T(8,128)(2,1)S(1)}, bf16[72,6144]{1,0:T(8,128)(2,1)S(1)}, u32[]{:S(2)}, u32[]{:S(2)}) collective-permute-start(bf16[72,6144]{1,0:T(8,128)(2,1)S(1)} %slice.187), channel_id=1, source_target_pairs={{0,1},{1,0},{2,3},{3,2},{4,5},{5,4},{6,7},{7,6},{8,9},{9,8},{10,11... | collective-permute-start | bytes 2654216 | tf_op jit(solution)/shard_map/ppermute | solution.py:167
  344.8 41.9 %collective-permute-start.23 = (bf16[40,6144]{1,0:T(8,128)(2,1)}, bf16[40,6144]{1,0:T(8,128)(2,1)S(1)}, u32[]{:S(2)}, u32[]{:S(2)}) collective-permute-start(bf16[40,6144]{1,0:T(8,128)(2,1)} %slice.178), channel_id=1, source_target_pairs={{0,4},{4,8},{8,12},{12,0},{1,5},{5,9},{9,13},{13,1},{2,6},{6,10},{... | collective-permute-start | bytes 1474568 | tf_op jit(solution)/shard_map/ppermute | solution.py:112
  349.4 12.4 %copy-start.19 = (bf16[72,6144]{1,0:T(8,128)(2,1)S(1)}, bf16[72,6144]{1,0:T(8,128)(2,1)}, u32[]{:S(2)}) copy-start(bf16[72,6144]{1,0:T(8,128)(2,1)} %copy-done.18) | copy-start | bytes 2654212
  349.4 12.3 %collective-permute-start.19 = (bf16[32,6144]{1,0:T(8,128)(2,1)S(1)}, bf16[32,6144]{1,0:T(8,128)(2,1)S(1)}, u32[]{:S(2)}, u32[]{:S(2)}) collective-permute-start(bf16[32,6144]{1,0:T(8,128)(2,1)S(1)} %copy-done.21), channel_id=1, source_target_pairs={{4,0},{8,4},{12,8},{0,12},{5,1},{9,5},{13,9},{1,13},{6,2},{10,6},{... | collective-permute-start | bytes 1179656 | tf_op jit(solution)/shard_map/ppermute | solution.py:111
  351.0 10.9 %copy-start.11 = (bf16[144,6144]{1,0:T(8,128)(2,1)S(1)}, bf16[144,6144]{1,0:T(8,128)(2,1)}, u32[]{:S(2)}) copy-start(bf16[144,6144]{1,0:T(8,128)(2,1)} %convolution_convert_fusion.1) | copy-start | bytes 5308420
  362.1 13.3 %collective-permute-start.36 = (bf16[32,6144]{1,0:T(8,128)(2,1)S(1)}, bf16[32,6144]{1,0:T(8,128)(2,1)S(1)}, u32[]{:S(2)}, u32[]{:S(2)}) collective-permute-start(bf16[32,6144]{1,0:T(8,128)(2,1)S(1)} %slice.188), channel_id=1, source_target_pairs={{4,0},{8,4},{12,8},{0,12},{5,1},{9,5},{13,9},{1,13},{6,2},{10,6},{... | collective-permute-start | bytes 1179656 | tf_op jit(solution)/shard_map/ppermute | solution.py:111
  362.9 53.0 %collective-permute-start.20 = (bf16[72,6144]{1,0:T(8,128)(2,1)S(1)}, bf16[72,6144]{1,0:T(8,128)(2,1)S(1)}, u32[]{:S(2)}, u32[]{:S(2)}) collective-permute-start(bf16[72,6144]{1,0:T(8,128)(2,1)S(1)} %pad_maximum_fusion.1), channel_id=1, source_target_pairs={{4,0},{8,4},{12,8},{0,12},{5,1},{9,5},{13,9},{1,13},{6,2},{10,6},{... | collective-permute-start | bytes 2654216 | tf_op jit(solution)/shard_map/ppermute | solution.py:115
  375.4 11.1 %collective-permute-start.40 = (bf16[40,6144]{1,0:T(8,128)(2,1)S(1)}, bf16[40,6144]{1,0:T(8,128)(2,1)S(1)}, u32[]{:S(2)}, u32[]{:S(2)}) collective-permute-start(bf16[40,6144]{1,0:T(8,128)(2,1)S(1)} %slice.194), channel_id=1, source_target_pairs={{0,4},{4,8},{8,12},{12,0},{1,5},{5,9},{9,13},{13,1},{2,6},{6,10},{... | collective-permute-start | bytes 1474568 | tf_op jit(solution)/shard_map/ppermute | solution.py:112
  375.6 14.4 %copy-start.17 = (bf16[72,6144]{1,0:T(8,128)(2,1)S(1)}, bf16[72,6144]{1,0:T(8,128)(2,1)}, u32[]{:S(2)}) copy-start(bf16[72,6144]{1,0:T(8,128)(2,1)} %copy-done.16) | copy-start | bytes 2654212
  386.5 25.0 %collective-permute-start.37 = (bf16[72,6144]{1,0:T(8,128)(2,1)S(1)}, bf16[72,6144]{1,0:T(8,128)(2,1)S(1)}, u32[]{:S(2)}, u32[]{:S(2)}) collective-permute-start(bf16[72,6144]{1,0:T(8,128)(2,1)S(1)} %pad_maximum_fusion.4), channel_id=1, source_target_pairs={{4,0},{8,4},{12,8},{0,12},{5,1},{9,5},{13,9},{1,13},{6,2},{10,6},{... | collective-permute-start | bytes 2654216 | tf_op jit(solution)/shard_map/ppermute | solution.py:115
  386.7 24.8 %copy-start.14 = (bf16[144,6144]{1,0:T(8,128)(2,1)S(1)}, bf16[144,6144]{1,0:T(8,128)(2,1)}, u32[]{:S(2)}) copy-start(bf16[144,6144]{1,0:T(8,128)(2,1)} %convolution_convert_fusion.3) | copy-start | bytes 5308420
  386.8 24.8 %collective-permute-start.41 = (bf16[72,6144]{1,0:T(8,128)(2,1)S(1)}, bf16[72,6144]{1,0:T(8,128)(2,1)S(1)}, u32[]{:S(2)}, u32[]{:S(2)}) collective-permute-start(bf16[72,6144]{1,0:T(8,128)(2,1)S(1)} %pad_maximum_fusion.5), channel_id=1, source_target_pairs={{0,4},{4,8},{8,12},{12,0},{1,5},{5,9},{9,13},{13,1},{2,6},{6,10},{... | collective-permute-start | bytes 2654216 | tf_op jit(solution)/shard_map/ppermute | solution.py:115
  390.3 44.3 %copy-start.12 = (bf16[144,6144]{1,0:T(8,128)(2,1)S(1)}, bf16[144,6144]{1,0:T(8,128)(2,1)}, u32[]{:S(2)}) copy-start(bf16[144,6144]{1,0:T(8,128)(2,1)} %convolution_convert_fusion.7) | copy-start | bytes 5308420
  390.3 32.6 %collective-permute-start.24 = (bf16[72,6144]{1,0:T(8,128)(2,1)S(1)}, bf16[72,6144]{1,0:T(8,128)(2,1)S(1)}, u32[]{:S(2)}, u32[]{:S(2)}) collective-permute-start(bf16[72,6144]{1,0:T(8,128)(2,1)S(1)} %pad_maximum_fusion.2), channel_id=1, source_target_pairs={{0,4},{4,8},{8,12},{12,0},{1,5},{5,9},{9,13},{13,1},{2,6},{6,10},{... | collective-permute-start | bytes 2654216 | tf_op jit(solution)/shard_map/ppermute | solution.py:115
  413.1 21.4 %collective-permute-start.42 = (bf16[72,6144]{1,0:T(8,128)(2,1)S(1)}, bf16[72,6144]{1,0:T(8,128)(2,1)S(1)}, u32[]{:S(2)}, u32[]{:S(2)}) collective-permute-start(bf16[72,6144]{1,0:T(8,128)(2,1)S(1)} %add_convert_fusion.1), channel_id=1, source_target_pairs={{0,2},{2,0},{1,3},{3,1},{4,6},{6,4},{5,7},{7,5},{8,10},{10,8},{9,1... | collective-permute-start | bytes 2654216 | tf_op jit(solution)/shard_map/ppermute | solution.py:168
  437.9 23.6 %all-to-all-start.3 = ((bf16[8,9,6144]{2,1,0:T(8,128)(2,1)}), bf16[8,9,6144]{2,1,0:T(8,128)(2,1)S(1)}, u32[]{:S(2)}, u32[]{:S(2)}) async-start(bf16[8,9,6144]{2,1,0:T(8,128)(2,1)} %reshape.168), calls=%async_computation.3 | async-start | bytes 3145728 | tf_op jit(solution)/shard_map/all_to_all | solution.py:169
  (13 other events, 37.4 us)
Sparse Core Ops, SparseCore 0:
  17.8 45.6 all-gather.1

commit v2 on v1

--- a/solution.py
+++ b/solution.py
@@ -1,6 +1,10 @@
+import functools
+
 import jax
 import jax.numpy as jnp
 from jax import lax
+from jax.experimental import pallas as pl
+from jax.experimental.pallas import tpu as pltpu
 from jax.sharding import Mesh, PartitionSpec as P
 
 HEAD_WIDTH = 128
@@ -90,29 +94,149 @@
     return columns.transpose(1, 0, 2).reshape(rows, NX * width)
 
 
-def expert_part(rows, w_gate, w_up, w_down):
-    gate_val = jnp.dot(rows, w_gate, preferred_element_type=jnp.float32)
-    up_val = jnp.dot(rows, w_up, preferred_element_type=jnp.float32)
-    hidden = (jax.nn.silu(gate_val) * up_val).astype(jnp.bfloat16)
-    return jnp.dot(hidden, w_down, preferred_element_type=jnp.float32).astype(jnp.bfloat16)
-
-
-def spread_z(own):
-    cut = own.shape[0] // 16 * 8
-    below = lax.ppermute(own, "z", UP)
-    above = lax.ppermute(own, "z", DOWN)
-    far_first = lax.ppermute(below[:cut], "z", UP)
-    far_second = lax.ppermute(above[cut:], "z", DOWN)
-    return own, below, above, jnp.concatenate([far_first, far_second], axis=0)
-
-
-def collect_z(own, below, above, far):
-    cut = own.shape[0] // 16 * 8
-    from_above = lax.ppermute(far[:cut], "z", DOWN)
-    from_below = lax.ppermute(far[cut:], "z", UP)
-    below = jnp.concatenate([add(below[:cut], from_above), below[cut:]], axis=0)
-    above = jnp.concatenate([above[:cut], add(above[cut:], from_below)], axis=0)
-    return add(own, lax.ppermute(below, "z", DOWN), lax.ppermute(above, "z", UP))
+def expert_kernel(count, core_ref, *refs):
+    own, other = refs[:count], refs[count : 2 * count]
+    gate_w, up_w, down_w = refs[2 * count : 2 * count + 3]
+    send, keep = refs[2 * count + 3 : 3 * count + 3], refs[3 * count + 3 : 4 * count + 3]
+    gate_sum, up_sum, hidden = refs[4 * count + 3 :]
+    step = pl.program_id(0)
+    high = own[0].shape[0]
+
+    def contract(parts, first):
+        for i, part in enumerate(parts):
+            at = pl.ds(i * high, high)
+            gate = jnp.dot(part[...], gate_w[...], preferred_element_type=jnp.float32)
+            up = jnp.dot(part[...], up_w[...], preferred_element_type=jnp.float32)
+            if first:
+                gate_sum[at], up_sum[at] = gate, up
+            else:
+                gate_sum[at] += gate
+                up_sum[at] += up
+
+    def expand(outs):
+        value = jnp.dot(hidden[...], down_w[...], preferred_element_type=jnp.float32)
+        for i, out in enumerate(outs):
+            out[...] = value[i * high : (i + 1) * high].astype(out.dtype)
+
+    @pl.when(step == 0)
+    def _():
+        contract(own, True)
+
+    @pl.when(step == 1)
+    def _():
+        contract(own, False)
+
+    @pl.when((step == 2) | (step == 3))
+    def _():
+        contract(other, False)
+
+    @pl.when(step == 3)
+    def _():
+        gate = gate_sum[...]
+        hidden[...] = (gate / (1.0 + jnp.exp(-gate)) * up_sum[...]).astype(hidden.dtype)
+
+    @pl.when((step == 4) | (step == 5))
+    def _():
+        expand(send)
+
+    @pl.when(step >= 6)
+    def _():
+        expand(keep)
+
+
+def expert_part(core, own, other, w_gate, w_up, w_down):
+    count = len(own)
+    high, half = own[0].shape
+    quarter = half // 2
+    units = w_gate.shape[1]
+
+    def place(first):
+        return pl.BlockSpec((high, quarter), lambda s, c: (0, jnp.clip(s - first, 0, 1)))
+
+    def in_quarter(s, c):
+        s = jnp.minimum(s, 3)
+        return jnp.where(s < 2, 2 * c[0] + s, 2 * (1 - c[0]) + s - 2)
+
+    def out_quarter(s, c):
+        s = jnp.maximum(s, 4) - 4
+        return jnp.where(s < 2, 2 * (1 - c[0]) + s, 2 * c[0] + s - 2)
+
+    rows = count * high
+    outs = pl.pallas_call(
+        functools.partial(expert_kernel, count),
+        grid_spec=pltpu.PrefetchScalarGridSpec(
+            num_scalar_prefetch=1,
+            grid=(8,),
+            in_specs=[place(0)] * count
+            + [place(2)] * count
+            + [
+                pl.BlockSpec((quarter, units), lambda s, c: (in_quarter(s, c), 0)),
+                pl.BlockSpec((quarter, units), lambda s, c: (in_quarter(s, c), 0)),
+                pl.BlockSpec((units, quarter), lambda s, c: (0, out_quarter(s, c))),
+            ],
+            out_specs=[place(4)] * count + [place(6)] * count,
+            scratch_shapes=[
+                pltpu.VMEM((rows, units), jnp.float32),
+                pltpu.VMEM((rows, units), jnp.float32),
+                pltpu.VMEM((rows, units), jnp.bfloat16),
+            ],
+        ),
+        out_shape=[jax.ShapeDtypeStruct((high, half), jnp.bfloat16)] * (2 * count),
+        compiler_params=pltpu.CompilerParams(vmem_limit_bytes=48 * 1024 * 1024),
+        cost_estimate=pl.CostEstimate(
+            flops=6 * rows * 2 * half * units,
+            bytes_accessed=12 * half * units + 8 * rows * half,
+            transcendentals=rows * units,
+        ),
+        name="expert_part",
+    )(core, *own, *other, w_gate, w_up, w_down)
+    return outs[:count], outs[count:]
+
+
+def after(value, *others):
+    return lax.optimization_barrier((value, *others))[0]
+
+
+def experts_of(own, w_gate, w_up, w_down):
+    cut = own.shape[0] // 32 * 16
+    c = lax.axis_index("c").astype(jnp.int32).reshape(1)
+
+    def run(*blocks):
+        other = [lax.ppermute(block, "c", SWAP) for block in blocks]
+        send, keep = expert_part(c, blocks, other, w_gate, w_up, w_down)
+        return [add(mine, lax.ppermute(his, "c", SWAP)) for mine, his in zip(keep, send)]
+
+    def near(block):
+        return lax.ppermute(block, "z", UP), lax.ppermute(block, "z", DOWN)
+
+    def far(below, above):
+        return jnp.concatenate(
+            [lax.ppermute(below[:cut], "z", UP), lax.ppermute(above[cut:], "z", DOWN)], axis=0
+        )
+
+    def far_back(block):
+        return lax.ppermute(block[:cut], "z", DOWN), lax.ppermute(block[cut:], "z", UP)
+
+    def near_back(below, above, from_above, from_below):
+        below = jnp.concatenate([add(below[:cut], from_above), below[cut:]], axis=0)
+        above = jnp.concatenate([above[:cut], add(above[cut:], from_below)], axis=0)
+        return lax.ppermute(below, "z", DOWN), lax.ppermute(above, "z", UP)
+
+    over = lax.ppermute(own, "yh", SWAP)
+    below, above = near(own)
+    far_own = far(below, above)
+    over_below, over_above = near(after(over, below, above))
+    far_over = far(over_below, over_above)
+    own, below, above = run(own, below, above)
+    far_own, over = run(far_own, over)
+    over_below, over_above = run(over_below, over_above)
+    (far_over,) = run(far_over)
+    own_far_back = far_back(far_own)
+    over_far_back = far_back(after(far_over, *own_far_back))
+    over_back = near_back(over_below, over_above, *over_far_back)
+    own_back = near_back(after(below, *over_back), above, *own_far_back)
+    over = lax.ppermute(add(over, *over_back), "yh", SWAP)
+    return add(own, *own_back, over)
 
 
 def per_device(
@@ -139,37 +263,51 @@
     logits = jnp.dot(normed.astype(jnp.float32), router, precision=lax.Precision.HIGHEST)
     experts = router.shape[1]
     rows = normed.shape[0]
-    cap = rows * 9 // 32
+    cap = 2 * rows * 9 // 32
     slots = experts * cap
-    hits = routes[:, :, None] == jnp.arange(experts, dtype=jnp.int32)
-    flat_hits = hits.astype(jnp.int32).reshape(rows * 2, experts)
+    c = lax.axis_index("c")
+    half = width // 2
+
+    def columns(array, core):
+        return lax.dynamic_slice_in_dim(array, core * half, half, axis=1)
+
+    def in_order(mine, his, axis):
+        return jnp.where(
+            c == 0,
+            jnp.concatenate([mine, his], axis=axis),
+            jnp.concatenate([his, mine], axis=axis),
+        )
+
+    pair_routes = in_order(routes, lax.ppermute(routes, "c", SWAP), 0)
+    pair_normed = in_order(columns(normed, c), lax.ppermute(columns(normed, 1 - c), "c", SWAP), 0)
+    rows2 = 2 * rows
+    hits = pair_routes[:, :, None] == jnp.arange(experts, dtype=jnp.int32)
+    flat_hits = hits.astype(jnp.int32).reshape(rows2 * 2, experts)
     before = jnp.cumsum(flat_hits, axis=0) - flat_hits
-    slot = jnp.sum(before.reshape(rows, 2, experts) * hits.astype(jnp.int32), axis=-1)
-    target = routes * cap + slot
+    slot = jnp.sum(before.reshape(rows2, 2, experts) * hits.astype(jnp.int32), axis=-1)
+    target = pair_routes * cap + slot
     placed = target[:, :, None] == jnp.arange(slots, dtype=jnp.int32)[None, None, :]
     chooser = jnp.any(placed, axis=1).astype(jnp.bfloat16).T
-    pair_logits = jnp.sum(jnp.where(hits, logits[:, None, :], 0.0), axis=-1)
+    own_hits = routes[:, :, None] == jnp.arange(experts, dtype=jnp.int32)
+    pair_logits = jnp.sum(jnp.where(own_hits, logits[:, None, :], 0.0), axis=-1)
     first_gate = 1.0 / (1.0 + jnp.exp(pair_logits[:, 1] - pair_logits[:, 0]))
     second_gate = 1.0 / (1.0 + jnp.exp(pair_logits[:, 0] - pair_logits[:, 1]))
-    gate_pair = jnp.stack([first_gate, second_gate], axis=1)
+    own_gates = jnp.stack([first_gate, second_gate], axis=1)
+    gate_pair = in_order(own_gates, lax.ppermute(own_gates, "c", SWAP), 0)
     combiner = jnp.sum(jnp.where(placed, gate_pair[:, :, None], 0.0), axis=1)
 
-    packed = jnp.dot(chooser, normed, preferred_element_type=jnp.float32).astype(jnp.bfloat16)
+    packed = jnp.dot(chooser, pair_normed, preferred_element_type=jnp.float32).astype(jnp.bfloat16)
     arrived = lax.all_to_all(
-        packed.reshape(experts, cap, width), ("x", "yl"), split_axis=0, concat_axis=0, tiled=True
-    ).reshape(slots, width)
-    over = lax.ppermute(arrived, "yh", SWAP)
-    blocks = spread_z(arrived) + spread_z(over)
-    sent = []
-    for block in blocks:
-        both = jnp.concatenate([block, lax.ppermute(block, "c", SWAP)], axis=0)
-        out = expert_part(both, w_gate, w_up, w_down)
-        sent.append(add(out[:slots], lax.ppermute(out[slots:], "c", SWAP)))
-    home = add(collect_z(*sent[:4]), lax.ppermute(collect_z(*sent[4:]), "yh", SWAP))
+        packed.reshape(experts, cap, half), ("x", "yl"), split_axis=0, concat_axis=0, tiled=True
+    ).reshape(slots, half)
+    home = experts_of(arrived, w_gate, w_up, w_down)
     returned = lax.all_to_all(
-        home.reshape(experts, cap, width), ("x", "yl"), split_axis=0, concat_axis=0, tiled=True
-    ).reshape(slots, width)
+        home.reshape(experts, cap, half), ("x", "yl"), split_axis=0, concat_axis=0, tiled=True
+    ).reshape(slots, half)
     mixture = jnp.dot(combiner, returned.astype(jnp.float32), precision=lax.Precision.HIGHEST)
+    mine = lax.dynamic_slice_in_dim(mixture, c * rows, rows, axis=0)
+    his = lax.dynamic_slice_in_dim(mixture, (1 - c) * rows, rows, axis=0)
+    mixture = in_order(mine, lax.ppermute(his, "c", SWAP), 1)
     return (resid + mixture).astype(jnp.bfloat16)
 
 

time: 482 us -> 393 us (0.82)
  the two profiles are of different devices: /device:TPU:96 before, /device:TPU:1 now
where the time goes in v2:
time: 393 us; the launch traced here: 388 us
  waiting for transfers between devices  147 us (37%)
  starting transfers between devices  107 us (27%)
  Pallas kernels  53.4 us (14%)
  other arithmetic  20.4 us (5%)
  blocking collectives  18.7 us (5%)
  matrix products  14.7 us (4%)
  between operations  14.5 us (4%)
  local copies, waits for them, and re-layouts  11.9 us (3%)
    pallas_call x4, Pallas kernels, expert_part(): pl.pallas_call(functools.partial(expert_kernel, count), grid_spec=pltpu.P...  53.4 us
    ppermute x4, waiting for transfers between devices, near_back(): return (lax.ppermute(below, 'z', DOWN), lax.ppermute(above, 'z', UP))  32.5 us
    ppermute x4, waiting for transfers between devices, near(): return (lax.ppermute(block, 'z', UP), lax.ppermute(block, 'z', DOWN))  26.6 us
    all_to_all x1, blocking collectives, per_device(): lax.all_to_all(packed.reshape(experts, cap, half), ('x', 'yl'), split_axi...  18.7 us
    ppermute x2, waiting for transfers between devices, far_back(): lax.ppermute(block[:cut], 'z', DOWN)  16.2 us
    ppermute x8, starting transfers between devices, run(): other = [lax.ppermute(block, 'c', SWAP) for block in blocks]  14.7 us
    ppermute x1, waiting for transfers between devices, gather_keys(): below = lax.ppermute(here, 'z', UP)  14.1 us
    ppermute x8, starting transfers between devices, run(): lax.ppermute(his, 'c', SWAP)  12.6 us
  transfers between devices with their start and end apart: 51, of which 27 were waited for; matrix products, arithmetic and copies ran while one was open for 8% of the time, Pallas kernels for 14%

profile of v2, /device:TPU:1, one launch (start us, length us, event | category | flops | bytes accessed | tf_op | source)
XLA Modules:
  0.0 387.8 jit_solution(1652695378560853095)
XLA Ops:
  9.6 3.9 %collective-permute-start = (bf16[272,128]{1,0:T(8,128)(2,1)S(1)}, bf16[272,128]{1,0:T(8,128)(2,1)S(1)}, u32[]{:S(2)}, u32[]{:S(2)}) collective-permute-start(bf16[272,128]{1,0:T(8,128)(2,1)S(1)} %pad_maximum_fusion.4), channel_id=1, source_target_pairs={{0,32},{32,64},{64,96},{1,33},{33,65},{65,97},{2,34},{34,66},{66,9... | collective-permute-start | bytes 208904 | tf_op jit(solution)/shard_map/ppermute | solution.py:30
  13.6 4.4 %collective-permute-start.1 = (bf16[272,128]{1,0:T(8,128)(2,1)S(1)}, bf16[272,128]{1,0:T(8,128)(2,1)S(1)}, u32[]{:S(2)}, u32[]{:S(2)}) collective-permute-start(bf16[272,128]{1,0:T(8,128)(2,1)S(1)} %pad_maximum_fusion.4), channel_id=1, source_target_pairs={{0,64},{32,96},{1,65},{33,97},{2,66},{34,98},{3,67},{35,99},{4,68}... | collective-permute-start | bytes 208904 | tf_op jit(solution)/shard_map/ppermute | solution.py:31
  19.3 1.4 collective-permute-start.2
  20.8 3.3 collective-permute-done.2
  24.1 1.7 collective-permute-start.3
  25.8 2.2 collective-permute-start.4
  28.9 14.1 %collective-permute-done.3 = bf16[1632,128]{1,0:T(8,128)(2,1)S(1)} collective-permute-done((bf16[1632,128]{1,0:T(8,128)(2,1)S(1)}, bf16[1632,128]{1,0:T(8,128)(2,1)S(1)}, u32[]{:S(2)}, u32[]{:S(2)}) %collective-permute-start.3) | collective-permute-done | bytes 417824 | tf_op jit(solution)/shard_map/ppermute | solution.py:35
  43.1 5.3 %collective-permute-done.4 = bf16[1632,128]{1,0:T(8,128)(2,1)S(1)} collective-permute-done((bf16[1632,128]{1,0:T(8,128)(2,1)S(1)}, bf16[1632,128]{1,0:T(8,128)(2,1)S(1)}, u32[]{:S(2)}, u32[]{:S(2)}) %collective-permute-start.4) | collective-permute-done | bytes 417824 | tf_op jit(solution)/shard_map/ppermute | solution.py:36
  48.5 4.5 %collective-permute-start.6 = (bf16[816,128]{1,0:T(8,128)(2,1)S(1)}, bf16[816,128]{1,0:T(8,128)(2,1)S(1)}, u32[]{:S(2)}, u32[]{:S(2)}) collective-permute-start(bf16[816,128]{1,0:T(8,128)(2,1)S(1)} %slice.95), channel_id=1, source_target_pairs={{4,0},{8,4},{12,8},{0,12},{5,1},{9,5},{13,9},{1,13},{6,2},{10,6},{... | collective-permute-start | bytes 626696 | tf_op jit(solution)/shard_map/ppermute | solution.py:39
  53.7 7.9 %collective-permute-done.6 = bf16[816,128]{1,0:T(8,128)(2,1)S(1)} collective-permute-done((bf16[816,128]{1,0:T(8,128)(2,1)S(1)}, bf16[816,128]{1,0:T(8,128)(2,1)S(1)}, u32[]{:S(2)}, u32[]{:S(2)}) %collective-permute-start.6) | collective-permute-done | bytes 208928 | tf_op jit(solution)/shard_map/ppermute | solution.py:39
  61.9 1.9 compare_and_fusion
  63.8 7.1 %fusion.40 = (f32[6,128]{1,0:T(8,128)S(1)}, bf16[6,128,3072]{1,2,0:T(8,128)(2,1)}) fusion(pred[128,3072]{0,1:T(8,128)(4,1)S(1)} %compare_and_fusion, bf16[3072,128,1]{1,0,2:T(8,128)(2,1)S(1)} %bitcast.78, bf16[128,6,128]{0,2,1:T(8,128)(2,1)} %bitcast.79), kind=kOutput, calls=%fused_computation.124 | convolution fusion | flops 1224477696 | bytes 6097920 | tf_op jit(solution)/shard_map/sub | solution.py:68
  70.9 3.2 fusion.19
  75.2 3.5 all-to-all-start
  78.7 8.5 %all-to-all-done = bf16[4,128,768]{2,1,0:T(8,128)(2,1)S(1)} async-done(((bf16[4,128,768]{2,1,0:T(8,128)(2,1)}), bf16[4,128,768]{2,1,0:T(8,128)(2,1)S(1)}, u32[]{:S(2)}, u32[]{:S(2)}) %all-to-all-start) | async-done | bytes 786464 | tf_op jit(solution)/shard_map/all_to_all | solution.py:83
  87.2 3.1 convolution_convert_fusion.1
  90.4 4.8 %collective-permute-start.7 = (bf16[4,2,32,1536]{3,2,1,0:T(8,128)(2,1)S(1)}, bf16[4,2,32,1536]{3,2,1,0:T(8,128)(2,1)S(1)}, u32[]{:S(2)}, u32[]{:S(2)}) collective-permute-start(bf16[4,2,32,1536]{3,2,1,0:T(8,128)(2,1)S(1)} %dynamic-slice_bitcast_fusion), channel_id=1, source_target_pairs={{0,1},{1,0},{2,3},{3,2},{4,5},{5,4},{6,7},{7,6},{8,9},{9,8},{10,11... | collective-permute-start | bytes 2359304 | tf_op jit(solution)/shard_map/ppermute | solution.py:89
  95.2 1.9 collective-permute-done.7
  97.3 4.2 %collective-permute-start.8 = (bf16[4,32,1536]{2,1,0:T(8,128)(2,1)S(1)}, bf16[4,32,1536]{2,1,0:T(8,128)(2,1)S(1)}, u32[]{:S(2)}, u32[]{:S(2)}) collective-permute-start(bf16[4,32,1536]{2,1,0:T(8,128)(2,1)S(1)} %dynamic-slice_bitcast_fusion.1), channel_id=1, source_target_pairs={{0,2},{2,0},{1,3},{3,1},{4,6},{6,4},{5,7},{7,5},{8,10},{10,8},{9,1... | collective-permute-start | bytes 1179656 | tf_op jit(solution)/shard_map/ppermute | solution.py:91
  103.4 7.4 %collective-permute-done.8 = bf16[4,32,1536]{2,1,0:T(8,128)(2,1)S(1)} collective-permute-done((bf16[4,32,1536]{2,1,0:T(8,128)(2,1)S(1)}, bf16[4,32,1536]{2,1,0:T(8,128)(2,1)S(1)}, u32[]{:S(2)}, u32[]{:S(2)}) %collective-permute-start.8) | collective-permute-done | bytes 393248 | tf_op jit(solution)/shard_map/ppermute | solution.py:91
  111.6 3.6 all-to-all-start.1
  116.0 6.1 %all-to-all-done.1 = bf16[4,32,1536]{2,1,0:T(8,128)(2,1)S(1)} async-done(((bf16[4,32,1536]{2,1,0:T(8,128)(2,1)}), bf16[4,32,1536]{2,1,0:T(8,128)(2,1)S(1)}, u32[]{:S(2)}, u32[]{:S(2)}) %all-to-all-start.1) | async-done | bytes 393248 | tf_op jit(solution)/shard_map/all_to_all | solution.py:93
  123.1 2.3 collective-permute-start.11
  127.2 18.7 %all_to_all.20 = bf16[8,18,3072]{2,1,0:T(8,128)(2,1)S(1)} all-to-all(bf16[8,18,3072]{2,1,0:T(8,128)(2,1)S(1)} %reshape.246), channel_id=1, replica_groups=mesh['x'=4,'yl'=2,'z'=4,'yh'=2,'c'=2] {'x','yl'}, dimensions={0} | all-to-all | bytes 1769472 | tf_op jit(solution)/shard_map/all_to_all | solution.py:300
  146.2 4.5 %collective-permute-start.13 = (bf16[144,3072]{1,0:T(8,128)(2,1)S(1)}, bf16[144,3072]{1,0:T(8,128)(2,1)S(1)}, u32[]{:S(2)}, u32[]{:S(2)}) collective-permute-start(bf16[144,3072]{1,0:T(8,128)(2,1)S(1)} %reshape.247.refs_0_), channel_id=1, source_target_pairs={{4,0},{8,4},{12,8},{0,12},{5,1},{9,5},{13,9},{1,13},{6,2},{10,6},{... | collective-permute-start | bytes 2654216 | tf_op jit(solution)/shard_map/ppermute | solution.py:210
  150.7 2.7 collective-permute-start.19
  153.4 14.7 %collective-permute-done.13.refs_2_ = bf16[144,3072]{1,0:T(8,128)(2,1)S(1)} collective-permute-done((bf16[144,3072]{1,0:T(8,128)(2,1)S(1)}, bf16[144,3072]{1,0:T(8,128)(2,1)S(1)}, u32[]{:S(2)}, u32[]{:S(2)}) %collective-permute-start.13) | collective-permute-done | bytes 884768 | tf_op jit(solution)/shard_map/ppermute | solution.py:210
  168.1 3.5 collective-permute-start.30
  171.8 2.7 collective-permute-start.21
  174.5 3.3 collective-permute-start.14
  177.8 3.0 collective-permute-done.29
  180.8 7.0 %collective-permute-start.15 = (bf16[144,3072]{1,0:T(8,128)(2,1)S(1)}, bf16[144,3072]{1,0:T(8,128)(2,1)S(1)}, u32[]{:S(2)}, u32[]{:S(2)}) collective-permute-start(bf16[144,3072]{1,0:T(8,128)(2,1)S(1)} %collective-permute-done.12.refs_1_), channel_id=1, source_target_pairs={{0,1},{1,0},{2,3},{3,2},{4,5},{5,4},{6,7},{7,6},{8,9},{9,8},{10,11... | collective-permute-start | bytes 2654216 | tf_op jit(solution)/shard_map/ppermute | solution.py:205
  187.8 11.9 %collective-permute-done.20.refs_0_ = bf16[144,3072]{1,0:T(8,128)(2,1)S(1)} collective-permute-done((bf16[144,3072]{1,0:T(8,128)(2,1)S(1)}, bf16[144,3072]{1,0:T(8,128)(2,1)S(1)}, u32[]{:S(2)}, u32[]{:S(2)}) %collective-permute-start.20) | collective-permute-done | bytes 884768 | tf_op jit(solution)/shard_map/ppermute | solution.py:210
  199.7 3.7 collective-permute-start.32
  203.7 2.6 collective-permute-start.26
  207.3 15.7 %expert_part.4 = (bf16[144,3072]{1,0:T(8,128)(2,1)S(1)}, bf16[144,3072]{1,0:T(8,128)(2,1)S(1)}, bf16[144,3072]{1,0:T(8,128)(2,1)S(1)}, bf16[144,3072]{1,0:T(8,12...) custom-call(s32[1]{0:T(128)} %bitcast.23.core_ref, bf16[144,3072]{1,0:T(8,128)(2,1)S(1)} %reshape.247.refs_0_, ...), custom_call_target="tpu_custom_call" | custom-call | flops 8153726976 | bytes 29491200 | tf_op jit(solution)/shard_map/expert_part/pallas_call | solution.py:165
  223.1 1.1 collective-permute-start.42
  224.3 9.3 %collective-permute-start.17 = (bf16[144,3072]{1,0:T(8,128)(2,1)S(1)}, bf16[144,3072]{1,0:T(8,128)(2,1)}, u32[]{:S(2)}, u32[]{:S(2)}) collective-permute-start(bf16[144,3072]{1,0:T(8,128)(2,1)S(1)} %get-tuple-element.25), channel_id=1, source_target_pairs={{0,1},{1,0},{2,3},{3,2},{4,5},{5,4},{6,7},{7,6},{8,9},{9,8},{10,11... | collective-permute-start | bytes 2654216 | tf_op jit(solution)/shard_map/ppermute | solution.py:207
  233.7 13.7 %expert_part.7 = (bf16[144,3072]{1,0:T(8,128)(2,1)}, bf16[144,3072]{1,0:T(8,128)(2,1)S(1)}, bf16[144,3072]{1,0:T(8,128)(2,1)S(1)}, bf16[144,3072]{1,0:T(8,128)(2,1)S(1)}) custom-call(s32[1]{0:T(128)} %bitcast.23.core_ref, bf16[144,3072]{1,0:T(8,128)(2,1)S(1)} %constant_dynamic-update-slice_fusion.23.refs_0_, ...), custom_call_target="tpu_custom_call" | custom-call | flops 5435817984 | bytes 25952256 | tf_op jit(solution)/shard_map/expert_part/pallas_call | solution.py:165
  247.9 1.1 constant_dynamic-update-slice_fusion.21.refs_0_
  249.1 1.4 add_convert_fusion.3
  252.2 13.1 %expert_part.5 = (bf16[144,3072]{1,0:T(8,128)(2,1)S(1)}, bf16[144,3072]{1,0:T(8,128)(2,1)S(1)}, bf16[144,3072]{1,0:T(8,128)(2,1)S(1)}, bf16[144,3072]{1,0:T(8,128)(2,1)S(1)}) custom-call(s32[1]{0:T(128)} %bitcast.23.core_ref, bf16[144,3072]{1,0:T(8,128)(2,1)S(1)} %collective-permute-done.20.refs_0_, bf16[144,3072]{1,0:T(8,128)(2,1)S(1)} %collective-permute-done.21.refs_1_, ...), custom_call_target="tpu_custom_call" | custom-call | flops 5435817984 | bytes 25952256 | tf_op jit(solution)/shard_map/expert_part/pallas_call | solution.py:165
  265.7 1.4 add_convert_fusion.8
  267.3 11.0 %expert_part.6 = (bf16[144,3072]{1,0:T(8,128)(2,1)S(1)}, bf16[144,3072]{1,0:T(8,128)(2,1)S(1)}) custom-call(s32[1]{0:T(128)} %bitcast.23.core_ref, bf16[144,3072]{1,0:T(8,128)(2,1)S(1)} %constant_dynamic-update-slice_fusion.21.refs_0_, bf16[144,3072]{1,0:T(8,128)(2,1)S(1)} %collective-permute-done.27.refs_1_, bf16[6144,512]{1,0:T(8,128)(2,1)} %refs_4_.5, ...), custom_call_target="tpu_custom_call" | custom-call | flops 2717908992 | bytes 22413312 | tf_op jit(solution)/shard_map/expert_part/pallas_call | solution.py:165
  279.0 1.4 add_convert_fusion.5
  282.6 8.7 %collective-permute-done.34 = bf16[64,3072]{1,0:T(8,128)(2,1)S(1)} collective-permute-done((bf16[64,3072]{1,0:T(8,128)(2,1)S(1)}, bf16[64,3072]{1,0:T(8,128)(2,1)S(1)}, u32[]{:S(2)}, u32[]{:S(2)}) %collective-permute-start.34) | collective-permute-done | bytes 393248 | tf_op jit(solution)/shard_map/ppermute | solution.py:218
  291.3 3.9 %collective-permute-done.35 = bf16[80,3072]{1,0:T(8,128)(2,1)S(1)} collective-permute-done((bf16[80,3072]{1,0:T(8,128)(2,1)S(1)}, bf16[80,3072]{1,0:T(8,128)(2,1)S(1)}, u32[]{:S(2)}, u32[]{:S(2)}) %collective-permute-start.35) | collective-permute-done | bytes 491552 | tf_op jit(solution)/shard_map/ppermute | solution.py:218
  295.6 1.5 collective-permute-start.39
  297.1 7.6 %collective-permute-done.36 = bf16[64,3072]{1,0:T(8,128)(2,1)S(1)} collective-permute-done((bf16[64,3072]{1,0:T(8,128)(2,1)S(1)}, bf16[64,3072]{1,0:T(8,128)(2,1)S(1)}, u32[]{:S(2)}, u32[]{:S(2)}) %collective-permute-start.36) | collective-permute-done | bytes 393248 | tf_op jit(solution)/shard_map/ppermute | solution.py:218
  304.9 1.6 collective-permute-start.37
  306.5 2.0 collective-permute-done.39
  310.5 13.4 %collective-permute-done.37 = bf16[144,3072]{1,0:T(8,128)(2,1)S(1)} collective-permute-done((bf16[144,3072]{1,0:T(8,128)(2,1)S(1)}, bf16[144,3072]{1,0:T(8,128)(2,1)S(1)}, u32[]{:S(2)}, u32[]{:S(2)}) %collective-permute-start.37) | collective-permute-done | bytes 884768 | tf_op jit(solution)/shard_map/ppermute | solution.py:223
  324.0 4.9 %collective-permute-done.40 = bf16[144,3072]{1,0:T(8,128)(2,1)S(1)} collective-permute-done((bf16[144,3072]{1,0:T(8,128)(2,1)S(1)}, bf16[144,3072]{1,0:T(8,128)(2,1)S(1)}, u32[]{:S(2)}, u32[]{:S(2)}) %collective-permute-start.40) | collective-permute-done | bytes 884768 | tf_op jit(solution)/shard_map/ppermute | solution.py:223
  328.9 2.7 add_convert_fusion.1
  331.6 2.7 collective-permute-start.45
  335.9 12.1 %collective-permute-done.43 = bf16[144,3072]{1,0:T(8,128)(2,1)} collective-permute-done((bf16[144,3072]{1,0:T(8,128)(2,1)}, bf16[144,3072]{1,0:T(8,128)(2,1)}, u32[]{:S(2)}, u32[]{:S(2)}) %collective-permute-start.43) | collective-permute-done | bytes 884768 | tf_op jit(solution)/shard_map/ppermute | solution.py:223
  348.9 2.0 collective-permute-done.41
  350.9 2.7 add_convert_fusion
  353.6 1.3 reshape.248
  354.9 3.6 all-to-all-start.3
  358.5 6.9 %collective-permute-start.10 = (f32[32,2]{0,1:T(2,128)S(1)}, f32[32,2]{0,1:T(2,128)S(1)}, u32[]{:S(2)}, u32[]{:S(2)}) collective-permute-start(f32[32,2]{0,1:T(2,128)S(1)} %pad_maximum_fusion.5), channel_id=1, source_target_pairs={{0,1},{1,0},{2,3},{3,2},{4,5},{5,4},{6,7},{7,6},{8,9},{9,8},{10,11... | collective-permute-start | bytes 776 | tf_op jit(solution)/shard_map/ppermute | solution.py:296
  366.8 2.8 all-to-all-done.3
  370.4 8.1 %collective-permute-start.46 = (f32[32,3072]{1,0:T(8,128)S(1)}, f32[32,3072]{1,0:T(8,128)S(1)}, u32[]{:S(2)}, u32[]{:S(2)}) collective-permute-start(f32[32,3072]{1,0:T(8,128)S(1)} %get-tuple-element.46), channel_id=1, source_target_pairs={{0,1},{1,0},{2,3},{3,2},{4,5},{5,4},{6,7},{7,6},{8,9},{9,8},{10,11... | collective-permute-start | bytes 1179656 | tf_op jit(solution)/shard_map/ppermute | solution.py:310
  378.5 1.3 collective-permute-done.46
  (188 shorter events, 30.0 us)
Async XLA Ops:
  6.5 328.9 %copy-start = (f32[6144,8]{0,1:T(8,128)S(1)}, f32[6144,8]{0,1:T(8,128)}, u32[]{:S(2)}) copy-start(f32[6144,8]{0,1:T(8,128)} %param.20) | copy-start | bytes 589828
  6.5 21.6 %copy-start.11 = (bf16[128,768]{1,0:T(8,128)(2,1)S(1)}, bf16[128,768]{1,0:T(8,128)(2,1)}, u32[]{:S(2)}) copy-start(bf16[128,768]{1,0:T(8,128)(2,1)} %param.14) | copy-start | bytes 589828
  6.5 80.7 %all-gather.2.cloned.1.call-start = ((), (), s32[]{:S(2)}) async-start(), calls=%async_computation.4 | async-start | bytes 2654208 | tf_op jit(solution)/shard_map/all_gather | solution.py:79
  9.6 9.2 %collective-permute-start = (bf16[272,128]{1,0:T(8,128)(2,1)S(1)}, bf16[272,128]{1,0:T(8,128)(2,1)S(1)}, u32[]{:S(2)}, u32[]{:S(2)}) collective-permute-start(bf16[272,128]{1,0:T(8,128)(2,1)S(1)} %pad_maximum_fusion.4), channel_id=1, source_target_pairs={{0,32},{32,64},{64,96},{1,33},{33,65},{65,97},{2,34},{34,66},{66,9... | collective-permute-start | bytes 208904 | tf_op jit(solution)/shard_map/ppermute | solution.py:30
  13.6 5.7 %collective-permute-start.1 = (bf16[272,128]{1,0:T(8,128)(2,1)S(1)}, bf16[272,128]{1,0:T(8,128)(2,1)S(1)}, u32[]{:S(2)}, u32[]{:S(2)}) collective-permute-start(bf16[272,128]{1,0:T(8,128)(2,1)S(1)} %pad_maximum_fusion.4), channel_id=1, source_target_pairs={{0,64},{32,96},{1,65},{33,97},{2,66},{34,98},{3,67},{35,99},{4,68}... | collective-permute-start | bytes 208904 | tf_op jit(solution)/shard_map/ppermute | solution.py:31
  19.3 4.7 %collective-permute-start.2 = (bf16[816,128]{1,0:T(8,128)(2,1)S(1)}, bf16[816,128]{1,0:T(8,128)(2,1)S(1)}, u32[]{:S(2)}, u32[]{:S(2)}) collective-permute-start(bf16[816,128]{1,0:T(8,128)(2,1)S(1)} %get-tuple-element.53), channel_id=1, source_target_pairs={{0,16},{16,0},{1,17},{17,1},{2,18},{18,2},{3,19},{19,3},{4,20},{20... | collective-permute-start | bytes 626696 | tf_op jit(solution)/shard_map/ppermute | solution.py:33
  24.1 18.9 %collective-permute-start.3 = (bf16[1632,128]{1,0:T(8,128)(2,1)S(1)}, bf16[1632,128]{1,0:T(8,128)(2,1)S(1)}, u32[]{:S(2)}, u32[]{:S(2)}) collective-permute-start(bf16[1632,128]{1,0:T(8,128)(2,1)S(1)} %get-tuple-element.49), channel_id=1, source_target_pairs={{0,4},{4,8},{8,12},{12,0},{1,5},{5,9},{9,13},{13,1},{2,6},{6,10},{... | collective-permute-start | bytes 1253384 | tf_op jit(solution)/shard_map/ppermute | solution.py:35
  25.8 22.7 %collective-permute-start.4 = (bf16[1632,128]{1,0:T(8,128)(2,1)S(1)}, bf16[1632,128]{1,0:T(8,128)(2,1)S(1)}, u32[]{:S(2)}, u32[]{:S(2)}) collective-permute-start(bf16[1632,128]{1,0:T(8,128)(2,1)S(1)} %get-tuple-element.49), channel_id=1, source_target_pairs={{4,0},{8,4},{12,8},{0,12},{5,1},{9,5},{13,9},{1,13},{6,2},{10,6},{... | collective-permute-start | bytes 1253384 | tf_op jit(solution)/shard_map/ppermute | solution.py:36
  43.0 10.6 %collective-permute-start.5 = (bf16[816,128]{1,0:T(8,128)(2,1)S(1)}, bf16[816,128]{1,0:T(8,128)(2,1)S(1)}, u32[]{:S(2)}, u32[]{:S(2)}) collective-permute-start(bf16[816,128]{1,0:T(8,128)(2,1)S(1)} %slice.94), channel_id=1, source_target_pairs={{0,4},{4,8},{8,12},{12,0},{1,5},{5,9},{9,13},{13,1},{2,6},{6,10},{... | collective-permute-start | bytes 626696 | tf_op jit(solution)/shard_map/ppermute | solution.py:38
  48.5 13.2 %collective-permute-start.6 = (bf16[816,128]{1,0:T(8,128)(2,1)S(1)}, bf16[816,128]{1,0:T(8,128)(2,1)S(1)}, u32[]{:S(2)}, u32[]{:S(2)}) collective-permute-start(bf16[816,128]{1,0:T(8,128)(2,1)S(1)} %slice.95), channel_id=1, source_target_pairs={{4,0},{8,4},{12,8},{0,12},{5,1},{9,5},{13,9},{1,13},{6,2},{10,6},{... | collective-permute-start | bytes 626696 | tf_op jit(solution)/shard_map/ppermute | solution.py:39
  53.7 8.2 %copy-start.15 = (s32[128]{0:T(128)S(1)}, s32[128]{0:T(128)}, u32[]{:S(2)}) copy-start(s32[128]{0:T(128)} %param.17) | copy-start | bytes 1540
  75.2 12.0 %all-to-all-start = ((bf16[4,128,768]{2,1,0:T(8,128)(2,1)}), bf16[4,128,768]{2,1,0:T(8,128)(2,1)S(1)}, u32[]{:S(2)}, u32[]{:S(2)}) async-start(bf16[4,128,768]{2,1,0:T(8,128)(2,1)} %broadcast_in_dim.83), calls=%async_computation | async-start | bytes 1572864 | tf_op jit(solution)/shard_map/all_to_all | solution.py:83
  90.4 11.2 %copy-start.14 = (s32[32,2]{0,1:T(2,128)S(1)}, s32[32,2]{0,1:T(2,128)}, u32[]{:S(2)}) copy-start(s32[32,2]{0,1:T(2,128)} %param.24) | copy-start | bytes 772
  90.4 6.7 %collective-permute-start.7 = (bf16[4,2,32,1536]{3,2,1,0:T(8,128)(2,1)S(1)}, bf16[4,2,32,1536]{3,2,1,0:T(8,128)(2,1)S(1)}, u32[]{:S(2)}, u32[]{:S(2)}) collective-permute-start(bf16[4,2,32,1536]{3,2,1,0:T(8,128)(2,1)S(1)} %dynamic-slice_bitcast_fusion), channel_id=1, source_target_pairs={{0,1},{1,0},{2,3},{3,2},{4,5},{5,4},{6,7},{7,6},{8,9},{9,8},{10,11... | collective-permute-start | bytes 2359304 | tf_op jit(solution)/shard_map/ppermute | solution.py:89
  97.3 13.4 %collective-permute-start.8 = (bf16[4,32,1536]{2,1,0:T(8,128)(2,1)S(1)}, bf16[4,32,1536]{2,1,0:T(8,128)(2,1)S(1)}, u32[]{:S(2)}, u32[]{:S(2)}) collective-permute-start(bf16[4,32,1536]{2,1,0:T(8,128)(2,1)S(1)} %dynamic-slice_bitcast_fusion.1), channel_id=1, source_target_pairs={{0,2},{2,0},{1,3},{3,1},{4,6},{6,4},{5,7},{7,5},{8,10},{10,8},{9,1... | collective-permute-start | bytes 1179656 | tf_op jit(solution)/shard_map/ppermute | solution.py:91
  101.6 1.5 collective-permute-start.9
  111.6 10.7 %copy-start.3 = (bf16[32,6144]{1,0:T(8,128)(2,1)S(1)}, bf16[32,6144]{1,0:T(8,128)(2,1)}, u32[]{:S(2)}) copy-start(bf16[32,6144]{1,0:T(8,128)(2,1)} %param.13) | copy-start | bytes 1179652
  111.6 10.5 %all-to-all-start.1 = ((bf16[4,32,1536]{2,1,0:T(8,128)(2,1)}), bf16[4,32,1536]{2,1,0:T(8,128)(2,1)S(1)}, u32[]{:S(2)}, u32[]{:S(2)}) async-start(bf16[4,32,1536]{2,1,0:T(8,128)(2,1)} %fusion.24), calls=%async_computation.1 | async-start | bytes 786432 | tf_op jit(solution)/shard_map/all_to_all | solution.py:93
  116.0 6.5 %copy-start.13 = (f32[6144]{0:T(1024)S(1)}, f32[6144]{0:T(1024)}, u32[]{:S(2)}) copy-start(f32[6144]{0:T(1024)} %param.19) | copy-start | bytes 73732
  122.7 3.8 copy-start.4
  123.1 3.4 collective-permute-start.11
  146.2 21.8 %collective-permute-start.13 = (bf16[144,3072]{1,0:T(8,128)(2,1)S(1)}, bf16[144,3072]{1,0:T(8,128)(2,1)S(1)}, u32[]{:S(2)}, u32[]{:S(2)}) collective-permute-start(bf16[144,3072]{1,0:T(8,128)(2,1)S(1)} %reshape.247.refs_0_), channel_id=1, source_target_pairs={{4,0},{8,4},{12,8},{0,12},{5,1},{9,5},{13,9},{1,13},{6,2},{10,6},{... | collective-permute-start | bytes 2654216 | tf_op jit(solution)/shard_map/ppermute | solution.py:210
  150.7 20.9 %collective-permute-start.12 = (bf16[144,3072]{1,0:T(8,128)(2,1)S(1)}, bf16[144,3072]{1,0:T(8,128)(2,1)S(1)}, u32[]{:S(2)}, u32[]{:S(2)}) collective-permute-start(bf16[144,3072]{1,0:T(8,128)(2,1)S(1)} %reshape.247.refs_0_), channel_id=1, source_target_pairs={{0,4},{4,8},{8,12},{12,0},{1,5},{5,9},{9,13},{13,1},{2,6},{6,10},{... | collective-permute-start | bytes 2654216 | tf_op jit(solution)/shard_map/ppermute | solution.py:210
  150.7 21.0 %collective-permute-start.19 = (bf16[144,3072]{1,0:T(8,128)(2,1)S(1)}, bf16[144,3072]{1,0:T(8,128)(2,1)S(1)}, u32[]{:S(2)}, u32[]{:S(2)}) collective-permute-start(bf16[144,3072]{1,0:T(8,128)(2,1)S(1)} %reshape.247.refs_0_), channel_id=1, source_target_pairs={{0,2},{2,0},{1,3},{3,1},{4,6},{6,4},{5,7},{7,5},{8,10},{10,8},{9,1... | collective-permute-start | bytes 2654216 | tf_op jit(solution)/shard_map/ppermute | solution.py:225
  168.1 35.4 %copy-start.10 = (bf16[144,3072]{1,0:T(8,128)(2,1)}, bf16[144,3072]{1,0:T(8,128)(2,1)S(1)}, u32[]{:S(2)}) copy-start(bf16[144,3072]{1,0:T(8,128)(2,1)S(1)} %collective-permute-done.13.refs_2_) | copy-start | bytes 2654212
  168.1 19.6 %collective-permute-start.30 = (bf16[80,3072]{1,0:T(8,128)(2,1)S(1)}, bf16[80,3072]{1,0:T(8,128)(2,1)S(1)}, u32[]{:S(2)}, u32[]{:S(2)}) collective-permute-start(bf16[80,3072]{1,0:T(8,128)(2,1)S(1)} %slice.103), channel_id=1, source_target_pairs={{4,0},{8,4},{12,8},{0,12},{5,1},{9,5},{13,9},{1,13},{6,2},{10,6},{... | collective-permute-start | bytes 1474568 | tf_op jit(solution)/shard_map/ppermute | solution.py:214
  171.6 32.0 %copy-start.12 = (bf16[144,3072]{1,0:T(8,128)(2,1)}, bf16[144,3072]{1,0:T(8,128)(2,1)S(1)}, u32[]{:S(2)}) copy-start(bf16[144,3072]{1,0:T(8,128)(2,1)S(1)} %collective-permute-done.12.refs_1_) | copy-start | bytes 2654212
  171.7 9.1 %collective-permute-start.29 = (bf16[64,3072]{1,0:T(8,128)(2,1)S(1)}, bf16[64,3072]{1,0:T(8,128)(2,1)S(1)}, u32[]{:S(2)}, u32[]{:S(2)}) collective-permute-start(bf16[64,3072]{1,0:T(8,128)(2,1)S(1)} %slice.102), channel_id=1, source_target_pairs={{0,4},{4,8},{8,12},{12,0},{1,5},{5,9},{9,13},{13,1},{2,6},{6,10},{... | collective-permute-start | bytes 1179656 | tf_op jit(solution)/shard_map/ppermute | solution.py:214
  171.7 28.0 %collective-permute-start.20 = (bf16[144,3072]{1,0:T(8,128)(2,1)S(1)}, bf16[144,3072]{1,0:T(8,128)(2,1)S(1)}, u32[]{:S(2)}, u32[]{:S(2)}) collective-permute-start(bf16[144,3072]{1,0:T(8,128)(2,1)S(1)} %collective-permute-done.19.refs_1_), channel_id=1, source_target_pairs={{0,4},{4,8},{8,12},{12,0},{1,5},{5,9},{9,13},{13,1},{2,6},{6,10},{... | collective-permute-start | bytes 2654216 | tf_op jit(solution)/shard_map/ppermute | solution.py:210
  171.8 31.6 %collective-permute-start.21 = (bf16[144,3072]{1,0:T(8,128)(2,1)S(1)}, bf16[144,3072]{1,0:T(8,128)(2,1)S(1)}, u32[]{:S(2)}, u32[]{:S(2)}) collective-permute-start(bf16[144,3072]{1,0:T(8,128)(2,1)S(1)} %collective-permute-done.19.refs_1_), channel_id=1, source_target_pairs={{4,0},{8,4},{12,8},{0,12},{5,1},{9,5},{13,9},{1,13},{6,2},{10,6},{... | collective-permute-start | bytes 2654216 | tf_op jit(solution)/shard_map/ppermute | solution.py:210
  174.5 29.1 %collective-permute-start.14 = (bf16[144,3072]{1,0:T(8,128)(2,1)S(1)}, bf16[144,3072]{1,0:T(8,128)(2,1)S(1)}, u32[]{:S(2)}, u32[]{:S(2)}) collective-permute-start(bf16[144,3072]{1,0:T(8,128)(2,1)S(1)} %reshape.247.refs_0_), channel_id=1, source_target_pairs={{0,1},{1,0},{2,3},{3,2},{4,5},{5,4},{6,7},{7,6},{8,9},{9,8},{10,11... | collective-permute-start | bytes 2654216 | tf_op jit(solution)/shard_map/ppermute | solution.py:205
  180.8 22.9 %collective-permute-start.15 = (bf16[144,3072]{1,0:T(8,128)(2,1)S(1)}, bf16[144,3072]{1,0:T(8,128)(2,1)S(1)}, u32[]{:S(2)}, u32[]{:S(2)}) collective-permute-start(bf16[144,3072]{1,0:T(8,128)(2,1)S(1)} %collective-permute-done.12.refs_1_), channel_id=1, source_target_pairs={{0,1},{1,0},{2,3},{3,2},{4,5},{5,4},{6,7},{7,6},{8,9},{9,8},{10,11... | collective-permute-start | bytes 2654216 | tf_op jit(solution)/shard_map/ppermute | solution.py:205
  187.7 18.6 %collective-permute-start.16 = (bf16[144,3072]{1,0:T(8,128)(2,1)S(1)}, bf16[144,3072]{1,0:T(8,128)(2,1)S(1)}, u32[]{:S(2)}, u32[]{:S(2)}) collective-permute-start(bf16[144,3072]{1,0:T(8,128)(2,1)S(1)} %collective-permute-done.13.refs_2_), channel_id=1, source_target_pairs={{0,1},{1,0},{2,3},{3,2},{4,5},{5,4},{6,7},{7,6},{8,9},{9,8},{10,11... | collective-permute-start | bytes 2654216 | tf_op jit(solution)/shard_map/ppermute | solution.py:205
  199.7 24.6 %collective-permute-start.32 = (bf16[144,3072]{1,0:T(8,128)(2,1)S(1)}, bf16[144,3072]{1,0:T(8,128)(2,1)S(1)}, u32[]{:S(2)}, u32[]{:S(2)}) collective-permute-start(bf16[144,3072]{1,0:T(8,128)(2,1)S(1)} %collective-permute-done.19.refs_1_), channel_id=1, source_target_pairs={{0,1},{1,0},{2,3},{3,2},{4,5},{5,4},{6,7},{7,6},{8,9},{9,8},{10,11... | collective-permute-start | bytes 2654216 | tf_op jit(solution)/shard_map/ppermute | solution.py:205
  203.5 30.1 %collective-permute-start.31 = (bf16[144,3072]{1,0:T(8,128)(2,1)S(1)}, bf16[144,3072]{1,0:T(8,128)(2,1)S(1)}, u32[]{:S(2)}, u32[]{:S(2)}) collective-permute-start(bf16[144,3072]{1,0:T(8,128)(2,1)S(1)} %constant_dynamic-update-slice_fusion.23.refs_0_), channel_id=1, source_target_pairs={{0,1},{1,0},{2,3},{3,2},{4,5},{5,4},{6,7},{7,6},{8,9},{9,8},{10,11... | collective-permute-start | bytes 2654216 | tf_op jit(solution)/shard_map/ppermute | solution.py:205
  203.6 20.5 %collective-permute-start.25 = (bf16[64,3072]{1,0:T(8,128)(2,1)S(1)}, bf16[64,3072]{1,0:T(8,128)(2,1)S(1)}, u32[]{:S(2)}, u32[]{:S(2)}) collective-permute-start(bf16[64,3072]{1,0:T(8,128)(2,1)S(1)} %slice.100), channel_id=1, source_target_pairs={{0,4},{4,8},{8,12},{12,0},{1,5},{5,9},{9,13},{13,1},{2,6},{6,10},{... | collective-permute-start | bytes 1179656 | tf_op jit(solution)/shard_map/ppermute | solution.py:214
  203.7 43.7 %collective-permute-start.26 = (bf16[80,3072]{1,0:T(8,128)(2,1)S(1)}, bf16[80,3072]{1,0:T(8,128)(2,1)}, u32[]{:S(2)}, u32[]{:S(2)}) collective-permute-start(bf16[80,3072]{1,0:T(8,128)(2,1)S(1)} %slice.101), channel_id=1, source_target_pairs={{4,0},{8,4},{12,8},{0,12},{5,1},{9,5},{13,9},{1,13},{6,2},{10,6},{... | collective-permute-start | bytes 1474568 | tf_op jit(solution)/shard_map/ppermute | solution.py:214
  223.1 25.9 %collective-permute-start.42 = (bf16[144,3072]{1,0:T(8,128)(2,1)S(1)}, bf16[144,3072]{1,0:T(8,128)(2,1)}, u32[]{:S(2)}, u32[]{:S(2)}) collective-permute-start(bf16[144,3072]{1,0:T(8,128)(2,1)S(1)} %get-tuple-element.40), channel_id=1, source_target_pairs={{0,1},{1,0},{2,3},{3,2},{4,5},{5,4},{6,7},{7,6},{8,9},{9,8},{10,11... | collective-permute-start | bytes 2654216 | tf_op jit(solution)/shard_map/ppermute | solution.py:207
  224.2 41.1 %collective-permute-start.18 = (bf16[144,3072]{1,0:T(8,128)(2,1)S(1)}, bf16[144,3072]{1,0:T(8,128)(2,1)}, u32[]{:S(2)}, u32[]{:S(2)}) collective-permute-start(bf16[144,3072]{1,0:T(8,128)(2,1)S(1)} %get-tuple-element.27), channel_id=1, source_target_pairs={{0,1},{1,0},{2,3},{3,2},{4,5},{5,4},{6,7},{7,6},{8,9},{9,8},{10,11... | collective-permute-start | bytes 2654216 | tf_op jit(solution)/shard_map/ppermute | solution.py:207
  224.3 9.3 %copy-start.8 = (bf16[144,3072]{1,0:T(8,128)(2,1)}, bf16[144,3072]{1,0:T(8,128)(2,1)S(1)}, u32[]{:S(2)}) copy-start(bf16[144,3072]{1,0:T(8,128)(2,1)S(1)} %collective-permute-done.32.refs_3_) | copy-start | bytes 2654212
  224.3 111.5 %collective-permute-start.17 = (bf16[144,3072]{1,0:T(8,128)(2,1)S(1)}, bf16[144,3072]{1,0:T(8,128)(2,1)}, u32[]{:S(2)}, u32[]{:S(2)}) collective-permute-start(bf16[144,3072]{1,0:T(8,128)(2,1)S(1)} %get-tuple-element.25), channel_id=1, source_target_pairs={{0,1},{1,0},{2,3},{3,2},{4,5},{5,4},{6,7},{7,6},{8,9},{9,8},{10,11... | collective-permute-start | bytes 2654216 | tf_op jit(solution)/shard_map/ppermute | solution.py:207
  233.6 16.9 %collective-permute-start.22 = (bf16[144,3072]{1,0:T(8,128)(2,1)S(1)}, bf16[144,3072]{1,0:T(8,128)(2,1)S(1)}, u32[]{:S(2)}, u32[]{:S(2)}) collective-permute-start(bf16[144,3072]{1,0:T(8,128)(2,1)S(1)} %collective-permute-done.20.refs_0_), channel_id=1, source_target_pairs={{0,1},{1,0},{2,3},{3,2},{4,5},{5,4},{6,7},{7,6},{8,9},{9,8},{10,11... | collective-permute-start | bytes 2654216 | tf_op jit(solution)/shard_map/ppermute | solution.py:205
  247.4 3.6 collective-permute-start.23
  248.9 18.2 %collective-permute-start.27 = (bf16[144,3072]{1,0:T(8,128)(2,1)S(1)}, bf16[144,3072]{1,0:T(8,128)(2,1)S(1)}, u32[]{:S(2)}, u32[]{:S(2)}) collective-permute-start(bf16[144,3072]{1,0:T(8,128)(2,1)S(1)} %constant_dynamic-update-slice_fusion.21.refs_0_), channel_id=1, source_target_pairs={{0,1},{1,0},{2,3},{3,2},{4,5},{5,4},{6,7},{7,6},{8,9},{9,8},{10,11... | collective-permute-start | bytes 2654216 | tf_op jit(solution)/shard_map/ppermute | solution.py:205
  250.5 14.8 %copy-start.6 = (bf16[144,3072]{1,0:T(8,128)(2,1)}, bf16[144,3072]{1,0:T(8,128)(2,1)S(1)}, u32[]{:S(2)}) copy-start(bf16[144,3072]{1,0:T(8,128)(2,1)S(1)} %add_convert_fusion.3) | copy-start | bytes 2654212
  250.5 27.8 %collective-permute-start.33 = (bf16[144,3072]{1,0:T(8,128)(2,1)}, bf16[144,3072]{1,0:T(8,128)(2,1)}, u32[]{:S(2)}, u32[]{:S(2)}) collective-permute-start(bf16[144,3072]{1,0:T(8,128)(2,1)} %get-tuple-element.34), channel_id=1, source_target_pairs={{0,1},{1,0},{2,3},{3,2},{4,5},{5,4},{6,7},{7,6},{8,9},{9,8},{10,11... | collective-permute-start | bytes 2654216 | tf_op jit(solution)/shard_map/ppermute | solution.py:207
  252.0 58.6 %collective-permute-start.44 = (bf16[144,3072]{1,0:T(8,128)(2,1)S(1)}, bf16[144,3072]{1,0:T(8,128)(2,1)}, u32[]{:S(2)}, u32[]{:S(2)}) collective-permute-start(bf16[144,3072]{1,0:T(8,128)(2,1)S(1)} %get-tuple-element.42), channel_id=1, source_target_pairs={{0,1},{1,0},{2,3},{3,2},{4,5},{5,4},{6,7},{7,6},{8,9},{9,8},{10,11... | collective-permute-start | bytes 2654216 | tf_op jit(solution)/shard_map/ppermute | solution.py:207
  265.2 15.2 %collective-permute-start.38 = (bf16[144,3072]{1,0:T(8,128)(2,1)S(1)}, bf16[144,3072]{1,0:T(8,128)(2,1)S(1)}, u32[]{:S(2)}, u32[]{:S(2)}) collective-permute-start(bf16[144,3072]{1,0:T(8,128)(2,1)S(1)} %get-tuple-element.37), channel_id=1, source_target_pairs={{0,1},{1,0},{2,3},{3,2},{4,5},{5,4},{6,7},{7,6},{8,9},{9,8},{10,11... | collective-permute-start | bytes 2654216 | tf_op jit(solution)/shard_map/ppermute | solution.py:207
  267.1 28.2 %collective-permute-start.24 = (bf16[144,3072]{1,0:T(8,128)(2,1)S(1)}, bf16[144,3072]{1,0:T(8,128)(2,1)S(1)}, u32[]{:S(2)}, u32[]{:S(2)}) collective-permute-start(bf16[144,3072]{1,0:T(8,128)(2,1)S(1)} %get-tuple-element.30), channel_id=1, source_target_pairs={{0,1},{1,0},{2,3},{3,2},{4,5},{5,4},{6,7},{7,6},{8,9},{9,8},{10,11... | collective-permute-start | bytes 2654216 | tf_op jit(solution)/shard_map/ppermute | solution.py:207
  278.3 3.2 collective-permute-start.28
  280.5 10.8 %collective-permute-start.34 = (bf16[64,3072]{1,0:T(8,128)(2,1)S(1)}, bf16[64,3072]{1,0:T(8,128)(2,1)S(1)}, u32[]{:S(2)}, u32[]{:S(2)}) collective-permute-start(bf16[64,3072]{1,0:T(8,128)(2,1)S(1)} %slice.104), channel_id=1, source_target_pairs={{4,0},{8,4},{12,8},{0,12},{5,1},{9,5},{13,9},{1,13},{6,2},{10,6},{... | collective-permute-start | bytes 1179656 | tf_op jit(solution)/shard_map/ppermute | solution.py:218
  281.5 13.7 %collective-permute-start.35 = (bf16[80,3072]{1,0:T(8,128)(2,1)S(1)}, bf16[80,3072]{1,0:T(8,128)(2,1)S(1)}, u32[]{:S(2)}, u32[]{:S(2)}) collective-permute-start(bf16[80,3072]{1,0:T(8,128)(2,1)S(1)} %slice.105), channel_id=1, source_target_pairs={{0,4},{4,8},{8,12},{12,0},{1,5},{5,9},{9,13},{13,1},{2,6},{6,10},{... | collective-permute-start | bytes 1474568 | tf_op jit(solution)/shard_map/ppermute | solution.py:218
  295.2 9.5 %collective-permute-start.36 = (bf16[64,3072]{1,0:T(8,128)(2,1)S(1)}, bf16[64,3072]{1,0:T(8,128)(2,1)S(1)}, u32[]{:S(2)}, u32[]{:S(2)}) collective-permute-start(bf16[64,3072]{1,0:T(8,128)(2,1)S(1)} %slice.85), channel_id=1, source_target_pairs={{4,0},{8,4},{12,8},{0,12},{5,1},{9,5},{13,9},{1,13},{6,2},{10,6},{... | collective-permute-start | bytes 1179656 | tf_op jit(solution)/shard_map/ppermute | solution.py:218
  295.6 12.8 %collective-permute-start.39 = (bf16[80,3072]{1,0:T(8,128)(2,1)S(1)}, bf16[80,3072]{1,0:T(8,128)(2,1)S(1)}, u32[]{:S(2)}, u32[]{:S(2)}) collective-permute-start(bf16[80,3072]{1,0:T(8,128)(2,1)S(1)} %slice.89), channel_id=1, source_target_pairs={{0,4},{4,8},{8,12},{12,0},{1,5},{5,9},{9,13},{13,1},{2,6},{6,10},{... | collective-permute-start | bytes 1474568 | tf_op jit(solution)/shard_map/ppermute | solution.py:218
  304.9 3.8 copy-start.7
  304.9 19.1 %collective-permute-start.37 = (bf16[144,3072]{1,0:T(8,128)(2,1)S(1)}, bf16[144,3072]{1,0:T(8,128)(2,1)S(1)}, u32[]{:S(2)}, u32[]{:S(2)}) collective-permute-start(bf16[144,3072]{1,0:T(8,128)(2,1)S(1)} %pad_maximum_fusion), channel_id=1, source_target_pairs={{4,0},{8,4},{12,8},{0,12},{5,1},{9,5},{13,9},{1,13},{6,2},{10,6},{... | collective-permute-start | bytes 2654216 | tf_op jit(solution)/shard_map/ppermute | solution.py:223
  308.6 20.3 %collective-permute-start.40 = (bf16[144,3072]{1,0:T(8,128)(2,1)S(1)}, bf16[144,3072]{1,0:T(8,128)(2,1)S(1)}, u32[]{:S(2)}, u32[]{:S(2)}) collective-permute-start(bf16[144,3072]{1,0:T(8,128)(2,1)S(1)} %pad_maximum_fusion.1), channel_id=1, source_target_pairs={{0,4},{4,8},{8,12},{12,0},{1,5},{5,9},{9,13},{13,1},{2,6},{6,10},{... | collective-permute-start | bytes 2654216 | tf_op jit(solution)/shard_map/ppermute | solution.py:223
  310.5 37.5 %collective-permute-start.43 = (bf16[144,3072]{1,0:T(8,128)(2,1)}, bf16[144,3072]{1,0:T(8,128)(2,1)}, u32[]{:S(2)}, u32[]{:S(2)}) collective-permute-start(bf16[144,3072]{1,0:T(8,128)(2,1)} %pad_maximum_fusion.3), channel_id=1, source_target_pairs={{0,4},{4,8},{8,12},{12,0},{1,5},{5,9},{9,13},{13,1},{2,6},{6,10},{... | collective-permute-start | bytes 2654216 | tf_op jit(solution)/shard_map/ppermute | solution.py:223
  331.6 17.3 %collective-permute-start.45 = (bf16[144,3072]{1,0:T(8,128)(2,1)}, bf16[144,3072]{1,0:T(8,128)(2,1)}, u32[]{:S(2)}, u32[]{:S(2)}) collective-permute-start(bf16[144,3072]{1,0:T(8,128)(2,1)} %add_convert_fusion.1), channel_id=1, source_target_pairs={{0,2},{2,0},{1,3},{3,1},{4,6},{6,4},{5,7},{7,5},{8,10},{10,8},{9,1... | collective-permute-start | bytes 2654216 | tf_op jit(solution)/shard_map/ppermute | solution.py:238
  335.4 15.5 %collective-permute-start.41 = (bf16[144,3072]{1,0:T(8,128)(2,1)}, bf16[144,3072]{1,0:T(8,128)(2,1)}, u32[]{:S(2)}, u32[]{:S(2)}) collective-permute-start(bf16[144,3072]{1,0:T(8,128)(2,1)} %pad_maximum_fusion.2), channel_id=1, source_target_pairs={{4,0},{8,4},{12,8},{0,12},{5,1},{9,5},{13,9},{1,13},{6,2},{10,6},{... | collective-permute-start | bytes 2654216 | tf_op jit(solution)/shard_map/ppermute | solution.py:223
  354.9 14.6 %all-to-all-start.3 = ((bf16[8,18,3072]{2,1,0:T(8,128)(2,1)}), bf16[8,18,3072]{2,1,0:T(8,128)(2,1)S(1)}, u32[]{:S(2)}, u32[]{:S(2)}) async-start(bf16[8,18,3072]{2,1,0:T(8,128)(2,1)} %reshape.248), calls=%async_computation.3 | async-start | bytes 2359296 | tf_op jit(solution)/shard_map/all_to_all | solution.py:304
  358.5 7.8 %collective-permute-start.10 = (f32[32,2]{0,1:T(2,128)S(1)}, f32[32,2]{0,1:T(2,128)S(1)}, u32[]{:S(2)}, u32[]{:S(2)}) collective-permute-start(f32[32,2]{0,1:T(2,128)S(1)} %pad_maximum_fusion.5), channel_id=1, source_target_pairs={{0,1},{1,0},{2,3},{3,2},{4,5},{5,4},{6,7},{7,6},{8,9},{9,8},{10,11... | collective-permute-start | bytes 776 | tf_op jit(solution)/shard_map/ppermute | solution.py:296
  369.8 10.0 %copy-start.2 = (f32[4,4,8,1536]{3,2,0,1:T(8,128)S(1)}, f32[4,4,8,1536]{3,2,0,1:T(8,128)}, u32[]{:S(2)}) copy-start(f32[4,4,8,1536]{3,2,0,1:T(8,128)} %copy-done.1) | copy-start | bytes 2359300
  370.4 9.4 %collective-permute-start.46 = (f32[32,3072]{1,0:T(8,128)S(1)}, f32[32,3072]{1,0:T(8,128)S(1)}, u32[]{:S(2)}, u32[]{:S(2)}) collective-permute-start(f32[32,3072]{1,0:T(8,128)S(1)} %get-tuple-element.46), channel_id=1, source_target_pairs={{0,1},{1,0},{2,3},{3,2},{4,5},{5,4},{6,7},{7,6},{8,9},{9,8},{10,11... | collective-permute-start | bytes 1179656 | tf_op jit(solution)/shard_map/ppermute | solution.py:310
  (7 other events, 13.0 us)
Sparse Core Ops, SparseCore 0:
  18.1 48.7 all-gather.1
